TPU v7x, 128 devices: a whole 4x4x4 slice. The times are simulated.
128 devices in a mesh: depth: 32 (over z, y_lo, x), head: 4 (over y_hi, core).
Axes of the slice: x: 4, y: 4 (y_hi: 2, y_lo: 2; y = y_hi * 2 + y_lo), z: 4, core: 2. Of those that a mesh axis runs over, the one named last changes fastest.
Arguments:
- embedded_homologs: bfloat16 [1024, 256, 768], P('depth'), may hold values from -6 to 6
- group_active_tallies: int32 [128], P('depth'), may hold values from 1 to 8
- asking_projector: bfloat16 [768, 768], P(None, 'head'), may hold values from -0.21875 to 0.21875
- lookup_projector: bfloat16 [768, 768], P(None, 'head'), may hold values from -0.21875 to 0.21875
- content_projector: bfloat16 [768, 768], P(None, 'head'), may hold values from -0.21875 to 0.21875
- contact_inner_matrix: float32 [12, 288], replicated, may hold values from -1.75 to 1.75
- contact_inner_offset: float32 [288], replicated, may hold values from -3 to 3
- contact_outer_matrix: float32 [288, 288], replicated, may hold values from -0.375 to 0.375
Outputs:
- attended: bfloat16 [1024, 256, 768], P('depth', None, 'head')
- pair: bfloat16 [256, 256, 288], P('head', 'depth')
All inputs are finite; a program needn't handle non-finite values.
Results may differ from a plain program's by a relative error of at most 0.0071.
Values may be sent and summed in bfloat16 or wider, within the bound.
A program may use at most 64 MiB of HBM per device.

v0:
```python
import jax
import jax.numpy as jnp
from jax import lax
from jax.sharding import PartitionSpec as P

HEAD_DIM = 64
BLOCK = 8


def project(merged_matrix, weight, homolog_sequences, sequence_extent):
    made = jnp.dot(merged_matrix, weight, preferred_element_type=jnp.float32).astype(jnp.bfloat16)
    return made.reshape(homolog_sequences, sequence_extent, weight.shape[1] // HEAD_DIM, HEAD_DIM)


def body(
    embedded_homologs,
    group_active_tallies,
    asking_projector,
    lookup_projector,
    content_projector,
    contact_inner_matrix,
    contact_inner_offset,
    contact_outer_matrix,
):
    homolog_sequences, sequence_extent, channel_extent = embedded_homologs.shape
    merged_matrix = embedded_homologs.reshape(homolog_sequences * sequence_extent, channel_extent)
    marked = (
        (jnp.arange(BLOCK, dtype=jnp.int32)[None, :] < group_active_tallies[:, None])
        .reshape(homolog_sequences)
        .astype(jnp.bfloat16)
    )
    query = (
        project(merged_matrix, asking_projector, homolog_sequences, sequence_extent)
        * marked[:, None, None, None]
    )
    key = project(merged_matrix, lookup_projector, homolog_sequences, sequence_extent)
    partial_logits = jnp.einsum("rihd,rjhd->hij", query, key, preferred_element_type=jnp.float32)
    count = lax.psum(jnp.sum(group_active_tallies.astype(jnp.float32)), "depth")
    scale = 1.0 / jnp.sqrt(HEAD_DIM * count)
    logits = lax.psum(partial_logits, "depth")
    maps = jax.nn.softmax(logits * scale, axis=-1).astype(jnp.bfloat16)
    value = project(merged_matrix, content_projector, homolog_sequences, sequence_extent)
    attended = jnp.einsum("hij,rjhd->rihd", maps, value, preferred_element_type=jnp.float32)
    attended = attended.astype(jnp.bfloat16).reshape(
        homolog_sequences, sequence_extent, content_projector.shape[1]
    )
    columns = sequence_extent // lax.axis_size("depth")
    begin = lax.axis_index("depth") * columns
    tile = lax.dynamic_slice_in_dim(maps, begin, columns, 2)
    regrouped = lax.all_to_all(tile, "head", split_axis=1, concat_axis=0, tiled=True)
    heads_all, tile_rows, tile_cols = regrouped.shape
    feature = (
        (sequence_extent * regrouped.astype(jnp.float32))
        .transpose(1, 2, 0)
        .reshape(tile_rows * tile_cols, heads_all)
    )
    hidden = jax.nn.gelu(
        jnp.dot(feature, contact_inner_matrix, precision=lax.Precision.HIGHEST)
        + contact_inner_offset
    )
    pair = jnp.dot(hidden, contact_outer_matrix, precision=lax.Precision.HIGHEST).astype(
        jnp.bfloat16
    )
    return (attended, pair.reshape(tile_rows, tile_cols, contact_outer_matrix.shape[1]))


def solution(mesh):
    return jax.shard_map(
        body,
        mesh=mesh,
        in_specs=(
            P("depth", None, None),
            P("depth"),
            P(None, "head"),
            P(None, "head"),
            P(None, "head"),
            P(),
            P(),
            P(),
        ),
        out_specs=(P("depth", None, "head"), P("head", "depth", None)),
        check_vma=False,
    )
```

profile of v0, /device:TPU:1, one launch (start us, length us, event | category | flops | bytes accessed | tf_op | source)
XLA Modules:
  0.0 373.5 jit_solution(15620526075372054954)
XLA Ops:
  7.2 0.0 copy-start
  7.2 0.0 all-reduce.2.cloned.1.call-start
  7.2 0.0 copy-start.1
  7.2 8.9 %convolution_convert_fusion.1 = bf16[8192,192]{0,1:T(8,128)(2,1)S(1)} fusion(bf16[8192,768]{1,0:T(8,128)(2,1)} %bitcast.62, bf16[768,192]{0,1:T(8,128)(2,1)} %param.10), kind=kOutput, calls=%fused_computation.2 | convolution fusion | flops 2417491968 | bytes 16023552 | tf_op jit(solution)/shard_map/dot_general | solution.py:11
  16.2 0.0 copy-start.2
  16.2 2.6 copy.50
  18.8 0.0 copy-done.1
  18.8 0.0 copy-done.2
  18.8 4.4 %convolution_convert_fusion = bf16[8192,192]{0,1:T(8,128)(2,1)S(1)} fusion(bf16[8192,768]{1,0:T(8,128)(2,1)S(1)} %bitcast.64, bf16[768,192]{0,1:T(8,128)(2,1)S(1)} %copy-done.2), kind=kOutput, calls=%fused_computation.1 | convolution fusion | flops 2417491968 | bytes 16023552 | tf_op jit(solution)/shard_map/dot_general | solution.py:11
  23.2 0.0 copy-start.6
  23.2 2.6 copy.51
  25.8 0.0 copy-done.6
  25.8 0.1 fusion.23
  25.9 0.1 reshape.58
  26.0 0.0 copy-start.3
  26.0 10.5 %fusion.10 = f32[3,256,256]{2,1,0:T(8,128)} fusion(bf16[32,256,3,64]{1,0,3,2:T(8,128)(2,1)} %bitcast.53, bf16[32,256,3,64]{1,0,3,2:T(8,128)(2,1)} %bitcast.52, bf16[32]{0:T(256)(128)(2,1)S(1)} %reshape.58), kind=kOutput, calls=%fused_computation.13 | convolution fusion | flops 806879232 | bytes 7077952 | tf_op jit(solution)/shard_map/rihd,rjhd->hij/dot_general | solution.py:37
  36.5 0.0 all-reduce.2.cloned.1.call-update
  36.5 0.6 convert_reduce_fusion
  37.1 72.0 %psum.15 = f32[]{:T(128)} all-reduce(f32[]{:T(128)} %convert_reduce_fusion), channel_id=1, replica_groups=mesh['depth'=32,'head'=4] {'depth'}, use_global_device_ids=true, to_apply=%region_2.0 | all-reduce | flops 1 | bytes 8 | tf_op jit(solution)/shard_map/psum | solution.py:38
  109.9 0.0 copy-done.3
  109.9 8.8 %convolution_convert_fusion.2 = bf16[8192,192]{0,1:T(8,128)(2,1)S(1)} fusion(bf16[8192,768]{1,0:T(8,128)(2,1)} %bitcast.63, bf16[768,192]{0,1:T(8,128)(2,1)S(1)} %copy-done.3), kind=kOutput, calls=%fused_computation.3 | convolution fusion | flops 2417491968 | bytes 16023552 | tf_op jit(solution)/shard_map/dot_general | solution.py:11
  118.7 2.6 copy.49
  121.3 204.6 %all-reduce.2.cloned.1.call-done = f32[3,256,256]{2,1,0:T(8,128)} async-done(((f32[3,256,256]{2,1,0:T(8,128)}), f32[3,256,256]{2,1,0:T(8,128)}) %all-reduce.2.cloned.1.call-update) | async-done | bytes 786448 | tf_op jit(solution)/shard_map/psum | solution.py:40
  325.9 1.4 fusion.24
  327.4 0.2 divide_convert_fusion
  327.5 0.1 constant_dynamic-slice_fusion
  327.7 0.2 copy.65
  327.9 0.8 reshape.61
  328.7 26.7 %all-to-all-start = ((bf16[4,2,768]{2,1,0:T(2,128)(2,1)}), bf16[4,2,768]{2,1,0:T(2,128)(2,1)S(1)}, u32[]{:S(2)}, u32[]{:S(2)}) async-start(bf16[4,2,768]{2,1,0:T(2,128)(2,1)} %reshape.61), calls=%async_computation | async-start | bytes 24576 | tf_op jit(solution)/shard_map/all_to_all | solution.py:50
  355.4 5.5 %convert_bitcast_fusion = bf16[32,256,3,64]{1,3,0,2:T(8,128)(2,1)S(1)} fusion(bf16[32,256,3,64]{1,0,3,2:T(8,128)(2,1)} %bitcast.51, bf16[3,256,256]{2,1,0:T(8,128)(2,1)S(1)} %divide_convert_fusion), kind=kOutput, calls=%fused_computation.9 | convolution fusion | flops 806879232 | bytes 6684672 | tf_op jit(solution)/shard_map/hij,rjhd->rihd/dot_general | solution.py:43
  360.9 0.0 copy-start.4
  360.9 0.0 copy-start.5
  360.9 1.9 copy.40
  362.8 0.0 all-to-all-done
  362.8 0.2 reshape.62
  363.1 0.1 copy.42
  363.2 0.1 mul.60
  363.3 0.2 copy.48
  363.5 0.2 reshape.56
  363.7 0.0 copy-done.4
  363.7 0.0 copy-done.5
  363.7 0.8 fusion.20
  364.6 0.0 copy-done
  364.6 1.2 convolution_convert_fusion.3
  365.8 0.9 copy.45
  (1 shorter events, 0.0 us)
Async XLA Ops:
  7.2 357.4 %copy-start = (f32[288,288]{1,0:T(8,128)S(1)}, f32[288,288]{1,0:T(8,128)}, u32[]{:S(2)}) copy-start(f32[288,288]{1,0:T(8,128)} %param.15) | copy-start | bytes 995332
  7.2 318.7 %all-reduce.2.cloned.1.call-start = ((), (), s32[]{:S(2)}) async-start(), calls=%async_computation.1 | async-start | bytes 1572864 | tf_op jit(solution)/shard_map/psum | solution.py:40
  7.2 11.6 %copy-start.1 = (bf16[32,256,768]{2,1,0:T(8,128)(2,1)S(1)}, bf16[32,256,768]{2,1,0:T(8,128)(2,1)}, u32[]{:S(2)}) copy-start(bf16[32,256,768]{2,1,0:T(8,128)(2,1)} %param.8) | copy-start | bytes 37748740
  16.2 2.6 copy-start.2
  23.2 2.6 copy-start.6
  26.0 83.9 %copy-start.3 = (bf16[768,192]{0,1:T(8,128)(2,1)S(1)}, bf16[768,192]{0,1:T(8,128)(2,1)}, u32[]{:S(2)}) copy-start(bf16[768,192]{0,1:T(8,128)(2,1)} %param.12) | copy-start | bytes 884740
  328.7 34.1 %all-to-all-start = ((bf16[4,2,768]{2,1,0:T(2,128)(2,1)}), bf16[4,2,768]{2,1,0:T(2,128)(2,1)S(1)}, u32[]{:S(2)}, u32[]{:S(2)}) async-start(bf16[4,2,768]{2,1,0:T(2,128)(2,1)} %reshape.61), calls=%async_computation | async-start | bytes 24576 | tf_op jit(solution)/shard_map/all_to_all | solution.py:50
  360.9 2.8 copy-start.4
  360.9 2.8 copy-start.5
Sparse Core Ops, SparseCore 0:
  36.7 289.1 all-reduce.1
where the time goes:
time: 374 us
  waiting for transfers between devices  205 us (55%)
  blocking collectives  72 us (19%)
  matrix products  40.2 us (11%)
  starting transfers between devices  26.7 us (7%)
  between operations  14.9 us (4%)
  local copies, waits for them, and re-layouts  12.8 us (3%)
    psum x1, waiting for transfers between devices, body(): logits = lax.psum(partial_logits, 'depth')  205 us
    psum x1, blocking collectives, body(): count = lax.psum(jnp.sum(group_active_tallies.astype(jnp.float32)), 'depth')  72 us
    all_to_all x1, starting transfers between devices, body(): lax.all_to_all(tile, 'head', split_axis=1, concat_axis=0, tiled=True)  26.7 us
    dot_general x3, matrix products, project(): jnp.dot(merged_matrix, weight, preferred_element_type=jnp.float32)  22.1 us
    dot_general x1, matrix products, body(): jnp.einsum('rihd,rjhd->hij', query, key, preferred_element_type=jnp.float32)  10.5 us
    unnamed x19, local copies, waits for them, and re-layouts  8.99 us
  transfers between devices with their start and end apart: 2, of which 1 were waited for; matrix products, arithmetic and copies ran while one was open for 5% of the time, Pallas kernels for 0%

commit v1 on v0

--- a/solution.py
+++ b/solution.py
@@ -35,10 +35,29 @@
     )
     key = project(merged_matrix, lookup_projector, homolog_sequences, sequence_extent)
     partial_logits = jnp.einsum("rihd,rjhd->hij", query, key, preferred_element_type=jnp.float32)
-    count = lax.psum(jnp.sum(group_active_tallies.astype(jnp.float32)), "depth")
+    groups = lax.axis_size("depth")
+    heads_here = partial_logits.shape[0]
+    rows = sequence_extent // groups
+    sent = (
+        partial_logits.reshape(heads_here, groups, rows, sequence_extent)
+        .transpose(1, 0, 2, 3)
+        .astype(jnp.bfloat16)
+        .reshape(groups, heads_here * rows, sequence_extent)
+    )
+    tally = jnp.sum(group_active_tallies.astype(jnp.float32)).astype(jnp.bfloat16)
+    sent = jnp.concatenate([sent, jnp.full((groups, 8, sequence_extent), tally, jnp.bfloat16)], axis=1)
+    got = lax.all_to_all(sent, "depth", split_axis=0, concat_axis=0, tiled=True)
+    total = jnp.sum(got.astype(jnp.float32), axis=0)
+    count = total[heads_here * rows, 0]
     scale = 1.0 / jnp.sqrt(HEAD_DIM * count)
-    logits = lax.psum(partial_logits, "depth")
-    maps = jax.nn.softmax(logits * scale, axis=-1).astype(jnp.bfloat16)
+    own = jax.nn.softmax(total[: heads_here * rows] * scale, axis=-1).astype(jnp.bfloat16)
+    own = jnp.broadcast_to(own[None], (groups,) + own.shape)
+    maps = lax.all_to_all(own, "depth", split_axis=0, concat_axis=0, tiled=True)
+    maps = (
+        maps.reshape(groups, heads_here, rows, sequence_extent)
+        .transpose(1, 0, 2, 3)
+        .reshape(heads_here, sequence_extent, sequence_extent)
+    )
     value = project(merged_matrix, content_projector, homolog_sequences, sequence_extent)
     attended = jnp.einsum("hij,rjhd->rihd", maps, value, preferred_element_type=jnp.float32)
     attended = attended.astype(jnp.bfloat16).reshape(

time: 374 us -> 92.8 us (0.25)
  waiting for transfers between devices: 205 us -> 0.01 us
  blocking collectives: 72 us -> 19.3 us
  starting transfers between devices: 26.7 us -> 11.3 us
  between operations: 14.9 us -> 1.52 us
  local copies, waits for them, and re-layouts: 12.8 us -> 16.8 us
    psum x1 -> x0, waiting for transfers between devices: 205 us -> none  [body(): logits = lax.psum(partial_logits, 'depth')]
    psum x1 -> x0, blocking collectives: 72 us -> none  [body(): count = lax.psum(jnp.sum(group_active_tallies.astype(jnp.float32)), 'depth')]
    all_to_all x1, starting transfers between devices: 26.7 us -> 6.16 us  [body(): lax.all_to_all(tile, 'head', split_axis=1, concat_axis=0, tiled=True)]
    all_to_all x0 -> x1, blocking collectives: none -> 19.3 us  [body(): got = lax.all_to_all(sent, 'depth', split_axis=0, concat_axis=0, tiled=True)]
    all_to_all x0 -> x1, starting transfers between devices: none -> 5.15 us  [body(): maps = lax.all_to_all(own, 'depth', split_axis=0, concat_axis=0, tiled=True)]
    unnamed x19 -> x17, local copies, waits for them, and re-layouts: 8.99 us -> 10.9 us
  transfers between devices with their start and end apart: 2 -> 2, of which waited for: 1 -> 0; matrix products, arithmetic and copies ran while one was open for 5% -> 24% of each run, Pallas kernels for 0% -> 0%
where the time goes in v1:
time: 92.8 us; the launch traced here: 92.3 us
  matrix products  40.9 us (44%)
  blocking collectives  19.3 us (21%)
  local copies, waits for them, and re-layouts  16.8 us (18%)
  starting transfers between devices  11.3 us (12%)
  other arithmetic  2.52 us (3%)
  between operations  1.52 us (2%)
    dot_general x3, matrix products, project(): jnp.dot(merged_matrix, weight, preferred_element_type=jnp.float32)  23.8 us
    all_to_all x1, blocking collectives, body(): got = lax.all_to_all(sent, 'depth', split_axis=0, concat_axis=0, tiled=True)  19.3 us
    unnamed x17, local copies, waits for them, and re-layouts  10.9 us
    dot_general x1, matrix products, body(): jnp.einsum('rihd,rjhd->hij', query, key, preferred_element_type=jnp.float32)  9.61 us
    all_to_all x1, starting transfers between devices, body(): lax.all_to_all(tile, 'head', split_axis=1, concat_axis=0, tiled=True)  6.16 us
    dot_general x1, matrix products, body(): jnp.einsum('hij,rjhd->rihd', maps, value, preferred_element_type=jnp.floa...  5.52 us
    all_to_all x1, starting transfers between devices, body(): maps = lax.all_to_all(own, 'depth', split_axis=0, concat_axis=0, tiled=True)  5.15 us
    convert_element_type x1, local copies, waits for them, and re-layouts, body(): attended.astype(jnp.bfloat16)  1.88 us
  transfers between devices with their start and end apart: 2, of which 0 were waited for; matrix products, arithmetic and copies ran while one was open for 24% of the time, Pallas kernels for 0%

profile of v1, /device:TPU:1, one launch (start us, length us, event | category | flops | bytes accessed | tf_op | source)
XLA Modules:
  0.0 92.3 jit_solution(15802920117377136241)
XLA Ops:
  0.6 0.0 copy-start
  0.6 0.8 fusion.27
  1.4 1.3 %convert_reduce_fusion.1 = bf16[]{:T(256)} fusion(s32[4]{0:T(128)} %param.9), kind=kLoop, calls=%fused_computation.36 | loop fusion | flops 7 | bytes 18 | tf_op jit(solution)/shard_map/reduce_sum | solution.py:47
  2.7 0.0 copy-start.1
  2.7 8.9 %convolution_convert_fusion.1 = bf16[8192,192]{0,1:T(8,128)(2,1)S(1)} fusion(bf16[8192,768]{1,0:T(8,128)(2,1)} %bitcast.86, bf16[768,192]{0,1:T(8,128)(2,1)} %param.10), kind=kOutput, calls=%fused_computation.1 | convolution fusion | flops 2417491968 | bytes 16023552 | tf_op jit(solution)/shard_map/dot_general | solution.py:11
  11.6 0.0 copy-start.2
  11.6 2.6 %copy.58 = bf16[24,8,32,256]{3,2,1,0:T(8,128)(2,1)} copy(bf16[24,8,32,256]{3,1,2,0:T(8,128)(2,1)S(1)} %bitcast.78) | data formatting | bytes 6291456
  14.3 0.0 copy-done.1
  14.3 0.0 copy-done.2
  14.3 4.4 %convolution_convert_fusion = bf16[8192,192]{0,1:T(8,128)(2,1)S(1)} fusion(bf16[8192,768]{1,0:T(8,128)(2,1)S(1)} %bitcast.88, bf16[768,192]{0,1:T(8,128)(2,1)S(1)} %copy-done.2), kind=kOutput, calls=%fused_computation | convolution fusion | flops 2417491968 | bytes 16023552 | tf_op jit(solution)/shard_map/dot_general | solution.py:11
  18.7 2.6 %copy.59 = bf16[24,8,32,256]{3,2,1,0:T(8,128)(2,1)} copy(bf16[24,8,32,256]{3,1,2,0:T(8,128)(2,1)S(1)} %bitcast.79) | data formatting | bytes 6291456
  21.3 0.1 reshape.76
  21.4 9.6 %fusion.13 = bf16[3,32,8,256]{3,2,1,0:T(8,128)(2,1)S(1)} fusion(bf16[32,256,3,64]{1,0,3,2:T(8,128)(2,1)} %bitcast.77, bf16[32,256,3,64]{1,0,3,2:T(8,128)(2,1)} %bitcast.76, bf16[32]{0:T(256)(128)(2,1)S(1)} %reshape.76), kind=kOutput, calls=%fused_computation.14 | convolution fusion | flops 807075840 | bytes 6684736 | tf_op jit(solution)/shard_map/rihd,rjhd->hij/dot_general | solution.py:37
  31.0 0.0 copy-start.3
  31.0 0.7 concatenate.3
  31.8 19.3 %all_to_all.19 = bf16[32,32,256]{2,1,0:T(8,128)(2,1)S(1)} all-to-all(bf16[32,32,256]{2,1,0:T(8,128)(2,1)S(1)} %concatenate.3), channel_id=1, replica_groups=mesh['depth'=32,'head'=4] {'depth'}, dimensions={0} | all-to-all | bytes 1048576 | tf_op jit(solution)/shard_map/all_to_all | solution.py:49
  51.1 0.1 convert_reduce_fusion
  51.2 0.5 slice.9
  52.4 0.1 fusion.26
  52.5 0.2 fusion.25
  52.7 0.1 divide_convert_fusion
  52.8 0.8 broadcast_in_dim.2
  53.6 5.1 %all-to-all-start.1 = ((bf16[32,24,256]{2,1,0:T(8,128)(2,1)}), bf16[32,24,256]{2,1,0:T(8,128)(2,1)S(1)}, u32[]{:S(2)}, u32[]{:S(2)}) async-start(bf16[32,24,256]{2,1,0:T(8,128)(2,1)} %broadcast_in_dim.2), calls=%async_computation.1 | async-start | bytes 786432 | tf_op jit(solution)/shard_map/all_to_all | solution.py:55
  58.7 0.0 copy-done.3
  58.7 10.4 %convolution_convert_fusion.2 = bf16[8192,192]{0,1:T(8,128)(2,1)} fusion(bf16[8192,768]{1,0:T(8,128)(2,1)} %bitcast.87, bf16[768,192]{0,1:T(8,128)(2,1)S(1)} %copy-done.3), kind=kOutput, calls=%fused_computation.2 | convolution fusion | flops 2417491968 | bytes 16023552 | tf_op jit(solution)/shard_map/dot_general | solution.py:11
  69.2 4.5 %copy.57 = bf16[24,8,32,256]{3,2,1,0:T(8,128)(2,1)} copy(bf16[24,8,32,256]{3,1,2,0:T(8,128)(2,1)} %bitcast.75) | data formatting | bytes 6291456
  73.7 0.0 all-to-all-done.1
  73.7 0.1 constant_dynamic-slice_fusion
  73.8 0.2 copy.88
  74.0 0.8 reshape.79
  74.9 6.2 %all-to-all-start.2 = ((bf16[4,2,768]{2,1,0:T(2,128)(2,1)}), bf16[4,2,768]{2,1,0:T(2,128)(2,1)S(1)}, u32[]{:S(2)}, u32[]{:S(2)}) async-start(bf16[4,2,768]{2,1,0:T(2,128)(2,1)} %reshape.79), calls=%async_computation.2 | async-start | bytes 24576 | tf_op jit(solution)/shard_map/all_to_all | solution.py:69
  81.0 5.5 %convert_bitcast_fusion = bf16[32,256,3,64]{1,3,0,2:T(8,128)(2,1)S(1)} fusion(bf16[32,256,3,64]{1,0,3,2:T(8,128)(2,1)} %bitcast.74, bf16[32,24,256]{2,1,0:T(8,128)(2,1)S(1)} %all-to-all-done.1), kind=kOutput, calls=%fused_computation.8 | convolution fusion | flops 806879232 | bytes 6684672 | tf_op jit(solution)/shard_map/hij,rjhd->rihd/dot_general | solution.py:62
  86.5 0.0 copy-start.4
  86.6 0.0 copy-start.5
  86.6 1.9 %copy.48 = bf16[32,256,3,64]{1,3,2,0:T(8,128)(2,1)} copy(bf16[32,256,3,64]{1,3,0,2:T(8,128)(2,1)S(1)} %convert_bitcast_fusion) | data formatting | bytes 6291456 | tf_op jit(solution)/shard_map/convert_element_type | solution.py:63
  88.5 0.0 all-to-all-done.2
  88.5 0.2 reshape.80
  88.7 0.1 copy.50
  88.8 0.1 mul.60
  89.0 0.2 copy.56
  89.1 0.2 reshape.74
  89.4 0.0 copy-done.4
  89.4 0.0 copy-done.5
  89.4 0.8 fusion.22
  90.2 0.0 copy-done
  90.2 1.2 %convolution_convert_fusion.3 = bf16[512,288]{0,1:T(8,128)(2,1)S(1)} fusion(f32[512,288]{0,1:T(8,128)S(1)} %fusion.22, f32[288,288]{1,0:T(8,128)S(1)} %copy-done), kind=kOutput, calls=%fused_computation.13 | convolution fusion | flops 509755392 | bytes 1216512 | tf_op jit(solution)/shard_map/dot_general | solution.py:80
  91.4 0.9 copy.53
  (3 shorter events, 0.1 us)
Async XLA Ops:
  0.6 89.6 %copy-start = (f32[288,288]{1,0:T(8,128)S(1)}, f32[288,288]{1,0:T(8,128)}, u32[]{:S(2)}) copy-start(f32[288,288]{1,0:T(8,128)} %param.15) | copy-start | bytes 995332
  2.7 11.6 %copy-start.1 = (bf16[32,256,768]{2,1,0:T(8,128)(2,1)S(1)}, bf16[32,256,768]{2,1,0:T(8,128)(2,1)}, u32[]{:S(2)}) copy-start(bf16[32,256,768]{2,1,0:T(8,128)(2,1)} %param.8) | copy-start | bytes 37748740
  11.6 2.6 %copy-start.2 = (bf16[768,192]{0,1:T(8,128)(2,1)S(1)}, bf16[768,192]{0,1:T(8,128)(2,1)}, u32[]{:S(2)}) copy-start(bf16[768,192]{0,1:T(8,128)(2,1)} %param.11) | copy-start | bytes 884740
  31.0 27.8 %copy-start.3 = (bf16[768,192]{0,1:T(8,128)(2,1)S(1)}, bf16[768,192]{0,1:T(8,128)(2,1)}, u32[]{:S(2)}) copy-start(bf16[768,192]{0,1:T(8,128)(2,1)} %param.12) | copy-start | bytes 884740
  53.6 20.1 %all-to-all-start.1 = ((bf16[32,24,256]{2,1,0:T(8,128)(2,1)}), bf16[32,24,256]{2,1,0:T(8,128)(2,1)S(1)}, u32[]{:S(2)}, u32[]{:S(2)}) async-start(bf16[32,24,256]{2,1,0:T(8,128)(2,1)} %broadcast_in_dim.2), calls=%async_computation.1 | async-start | bytes 786432 | tf_op jit(solution)/shard_map/all_to_all | solution.py:55
  74.9 13.6 %all-to-all-start.2 = ((bf16[4,2,768]{2,1,0:T(2,128)(2,1)}), bf16[4,2,768]{2,1,0:T(2,128)(2,1)S(1)}, u32[]{:S(2)}, u32[]{:S(2)}) async-start(bf16[4,2,768]{2,1,0:T(2,128)(2,1)} %reshape.79), calls=%async_computation.2 | async-start | bytes 24576 | tf_op jit(solution)/shard_map/all_to_all | solution.py:69
  86.5 2.8 %copy-start.4 = (f32[12,288]{1,0:T(8,128)S(1)}, f32[12,288]{1,0:T(8,128)}, u32[]{:S(2)}) copy-start(f32[12,288]{1,0:T(8,128)} %param.13) | copy-start | bytes 41476
  86.6 2.8 %copy-start.5 = (f32[288]{0:T(512)S(1)}, f32[288]{0:T(512)}, u32[]{:S(2)}) copy-start(f32[288]{0:T(512)} %param.14) | copy-start | bytes 3460

commit v2 on v0

v2 whole, which is shorter than its diff:
```python
import functools

import jax
import jax.numpy as jnp
from jax import lax
from jax.experimental import pallas as pl
from jax.experimental.pallas import tpu as pltpu
from jax.sharding import PartitionSpec as P

HEAD_DIM = 64
BLOCK = 8
LANES = 128
CHUNK = 4

NT = (((1,), (1,)), ((), ()))
TN = (((0,), (0,)), ((), ()))
F32 = jnp.float32
BF16 = jnp.bfloat16


def dot(a, b, dims):
    return lax.dot_general(a, b, dims, preferred_element_type=F32)


def split_words(a):
    high = a.astype(BF16)
    return high, (a - high.astype(F32)).astype(BF16)


def kernel(
    groups,
    teams,
    tallies,
    x_hbm,
    wq_hbm,
    wk_hbm,
    wv_hbm,
    inner,
    offset,
    outer,
    attended,
    pair,
    x,
    w,
    qs,
    ks,
    vs,
    sums,
    sums_in,
    maps_all,
    counts,
    tile_out,
    tile_in,
    x_sem,
    w_sem,
    count_sem,
    sum_sem,
    map_sem,
    tile_send,
    tile_recv,
):
    rows, sites, width = x.shape
    made = w.shape[0] // 3
    heads = made // HEAD_DIM
    own_rows = sites // groups
    me = lax.axis_index("depth")
    team = lax.axis_index("head")
    steps = rows // CHUNK

    def x_copy(c):
        part = pl.ds(c * CHUNK, CHUNK)
        return pltpu.make_async_copy(x_hbm.at[part], x.at[part], x_sem.at[c])

    def w_copy(n):
        return pltpu.make_async_copy(
            (wq_hbm, wk_hbm, wv_hbm)[n], w.at[pl.ds(n * made, made)], w_sem.at[n]
        )

    w_copy(0).start()
    w_copy(1).start()
    for c in range(steps):
        x_copy(c).start()
    w_copy(2).start()

    barrier = pltpu.get_barrier_semaphore()

    def greet(k, carry):
        pl.semaphore_signal(barrier, inc=1, device_id=(lax.rem(me + k, groups), team), device_id_type=pl.DeviceIdType.MESH)
        return carry

    lax.fori_loop(1, groups, greet, 0)
    for k in range(1, teams):
        pl.semaphore_signal(barrier, inc=1, device_id=(me, lax.rem(team + k, teams)), device_id_type=pl.DeviceIdType.MESH)

    w_copy(0).wait()
    w_copy(1).wait()

    def project_qk(c, carry):
        x_copy(c).wait()
        for n in range(CHUNK):
            r = c * CHUNK + n
            live = jnp.where(lax.rem(r, BLOCK) < tallies[r // BLOCK], 1.0, 0.0)
            qk = dot(w[: 2 * made], x[r], NT)
            q = (qk[:made] * live).astype(BF16)
            k = qk[made:].astype(BF16)
            for h in range(heads):
                place = pl.ds(r * HEAD_DIM, HEAD_DIM)
                qs[h, place, :] = q[h * HEAD_DIM : (h + 1) * HEAD_DIM]
                ks[h, place, :] = k[h * HEAD_DIM : (h + 1) * HEAD_DIM]
        return carry

    lax.fori_loop(0, steps, project_qk, 0)

    count = jnp.float32(0)
    for n in range(rows // BLOCK):
        count += tallies[n].astype(F32)
    counts[me] = jnp.full(counts.shape[1:], count, F32)
    pl.semaphore_wait(barrier, groups - 1 + teams - 1)

    def count_copy(k):
        return pltpu.make_async_remote_copy(
            src_ref=counts.at[me],
            dst_ref=counts.at[me],
            send_sem=count_sem.at[0],
            recv_sem=count_sem.at[1],
            device_id=(lax.rem(me + k, groups), team),
            device_id_type=pl.DeviceIdType.MESH,
        )

    lax.fori_loop(1, groups, lambda k, carry: (count_copy(k).start(), carry)[1], 0)

    for h in range(heads):
        logits = dot(qs[h], ks[h], TN)
        halves = [
            logits[:, n * LANES : (n + 1) * LANES].reshape(groups, own_rows, LANES)
            for n in range(sites // LANES)
        ]
        deep = own_rows * len(halves)
        sums[:, h * deep : (h + 1) * deep, :] = jnp.concatenate(halves, axis=1).astype(BF16)

    def sum_copy(k):
        to = lax.rem(me + k, groups)
        return pltpu.make_async_remote_copy(
            src_ref=sums.at[to],
            dst_ref=sums_in.at[k - 1],
            send_sem=sum_sem.at[0],
            recv_sem=sum_sem.at[1],
            device_id=(to, team),
            device_id_type=pl.DeviceIdType.MESH,
        )

    lax.fori_loop(1, groups, lambda k, carry: (sum_copy(k).start(), carry)[1], 0)

    w_copy(2).wait()

    def project_v(c, carry):
        for n in range(CHUNK):
            r = c * CHUNK + n
            v = dot(w[2 * made :], x[r], NT).astype(BF16)
            for h in range(heads):
                vs[h, pl.ds(r * HEAD_DIM, HEAD_DIM), :] = v[h * HEAD_DIM : (h + 1) * HEAD_DIM]
        return carry

    lax.fori_loop(0, steps, project_v, 0)

    def wait_all(buffer, sem):
        most = buffer.at[pl.ds(0, groups - 1)]
        pltpu.make_async_copy(most, most, sem).wait()

    wait_all(counts, count_sem.at[1])
    wait_all(sums_in, sum_sem.at[1])
    total_count = jnp.sum(counts[...], axis=0)[:1, :1]
    scale = lax.rsqrt(HEAD_DIM * total_count)
    total = sums[me].astype(F32) + jnp.sum(sums_in[...].astype(F32), axis=0)
    deep = own_rows * (sites // LANES)
    blocks = []
    for h in range(heads):
        part = total[h * deep : (h + 1) * deep] * scale
        left, right = part[:own_rows], part[own_rows:]
        top = jnp.maximum(jnp.max(left, axis=1, keepdims=True), jnp.max(right, axis=1, keepdims=True))
        left, right = jnp.exp(left - top), jnp.exp(right - top)
        whole = jnp.sum(left, axis=1, keepdims=True) + jnp.sum(right, axis=1, keepdims=True)
        blocks += [left / whole, right / whole]
    maps_all[me] = jnp.concatenate(blocks, axis=0).astype(BF16)

    def map_copy(k):
        return pltpu.make_async_remote_copy(
            src_ref=maps_all.at[me],
            dst_ref=maps_all.at[me],
            send_sem=map_sem.at[0],
            recv_sem=map_sem.at[1],
            device_id=(lax.rem(me + k, groups), team),
            device_id_type=pl.DeviceIdType.MESH,
        )

    lax.fori_loop(1, groups, lambda k, carry: (map_copy(k).start(), carry)[1], 0)

    wait_all(maps_all, map_sem.at[1])
    maps = []
    for h in range(heads):
        part = maps_all[:, h * deep : (h + 1) * deep, :].astype(F32)
        maps.append(
            jnp.concatenate(
                [part[:, :own_rows].reshape(sites, LANES), part[:, own_rows:].reshape(sites, LANES)], axis=1
            ).astype(BF16)
        )

    column = lax.broadcasted_iota(jnp.int32, (sites, LANES), 0) - me * own_rows
    lane = lax.broadcasted_iota(jnp.int32, (sites, LANES), 1)
    tile = jnp.zeros((sites, LANES), F32)
    for h in range(heads):
        place = lane - (team * heads + h) * own_rows
        pick = (place == column) & (place >= 0) & (place < own_rows)
        tile += dot(maps[h], pick.astype(F32).astype(BF16), (((1,), (0,)), ((), ())))
    tile_out[...] = tile.astype(BF16).reshape(tile_out.shape)

    def tile_copy(k):
        to = lax.rem(team + k, teams)
        return pltpu.make_async_remote_copy(
            src_ref=tile_out.at[to],
            dst_ref=tile_in.at[k - 1],
            send_sem=tile_send.at[k - 1],
            recv_sem=tile_recv.at[k - 1],
            device_id=(me, to),
            device_id_type=pl.DeviceIdType.MESH,
        )

    for k in range(1, teams):
        tile_copy(k).start()

    for h in range(heads):
        right = maps[h]

        def apply(c, carry):
            place = pl.ds(pl.multiple_of(c * 8 * HEAD_DIM, 8 * HEAD_DIM), 8 * HEAD_DIM)
            out = dot(vs[h, place, :], right, NT).astype(BF16)
            attended[pl.ds(c * 8, 8), h * HEAD_DIM : (h + 1) * HEAD_DIM, :] = out.reshape(8, HEAD_DIM, sites)
            return carry

        lax.fori_loop(0, rows // 8, apply, 0)

    inner_rows = jnp.concatenate(
        [
            jnp.broadcast_to(inner[...][:, None, :], (inner.shape[0], own_rows, inner.shape[1])).reshape(
                inner.shape[0] * own_rows, inner.shape[1]
            ),
            jnp.zeros((LANES - inner.shape[0] * own_rows, inner.shape[1]), F32),
        ],
        axis=0,
    )
    inner_high, inner_low = split_words(inner_rows)
    outer_high, outer_low = split_words(outer[...])
    for k in range(1, teams):
        tile_copy(k).wait_recv()
    tile_sites = sites // teams
    flat = tile_out[team].astype(F32)
    for k in range(1, teams):
        flat += tile_in[k - 1].astype(F32)
    spread = jnp.broadcast_to((flat * sites)[:, None, :], (tile_sites, own_rows, LANES))
    keep = lax.rem(lax.broadcasted_iota(jnp.int32, (tile_sites, own_rows, LANES), 2), own_rows) == (
        lax.broadcasted_iota(jnp.int32, (tile_sites, own_rows, LANES), 1)
    )
    feature = jnp.where(keep, spread, 0.0).reshape(tile_sites * own_rows, LANES).astype(BF16)
    plain = (((1,), (0,)), ((), ()))
    before = dot(feature, inner_high, plain) + dot(feature, inner_low, plain) + offset[...]
    hidden_high, hidden_low = split_words(jax.nn.gelu(before))
    pair[...] = (
        dot(hidden_high, outer_high, plain)
        + dot(hidden_low, outer_high, plain)
        + dot(hidden_high, outer_low, plain)
    ).astype(BF16)

    for k in range(1, teams):
        tile_copy(k).wait_send()
    wait_all(counts, count_sem.at[0])
    wait_all(sums_in, sum_sem.at[0])
    wait_all(maps_all, map_sem.at[0])


def body(
    embedded_homologs,
    group_active_tallies,
    asking_projector,
    lookup_projector,
    content_projector,
    contact_inner_matrix,
    contact_inner_offset,
    contact_outer_matrix,
):
    rows, sites, width = embedded_homologs.shape
    made = asking_projector.shape[1]
    heads = made // HEAD_DIM
    groups, teams = lax.axis_size("depth"), lax.axis_size("head")
    own_rows = sites // groups
    features = contact_inner_matrix.shape[1]
    outputs = contact_outer_matrix.shape[1]
    deep = heads * own_rows * (sites // LANES)
    tile_rows = sites // teams
    anywhere = pl.BlockSpec(memory_space=pl.ANY)
    local = pl.BlockSpec(memory_space=pltpu.VMEM)
    attended, pair = pl.pallas_call(
        functools.partial(kernel, groups, teams),
        out_shape=(
            jax.ShapeDtypeStruct((rows, made, sites), BF16),
            jax.ShapeDtypeStruct((tile_rows * own_rows, outputs), BF16),
        ),
        in_specs=[pl.BlockSpec(memory_space=pltpu.SMEM)] + [anywhere] * 4 + [local] * 3,
        out_specs=(local, local),
        scratch_shapes=[
            pltpu.VMEM((rows, sites, width), BF16),
            pltpu.VMEM((3 * made, width), BF16),
            pltpu.VMEM((heads, rows * HEAD_DIM, sites), BF16),
            pltpu.VMEM((heads, rows * HEAD_DIM, sites), BF16),
            pltpu.VMEM((heads, rows * HEAD_DIM, sites), BF16),
            pltpu.VMEM((groups, deep, LANES), BF16),
            pltpu.VMEM((groups - 1, deep, LANES), BF16),
            pltpu.VMEM((groups, deep, LANES), BF16),
            pltpu.VMEM((groups, 8, LANES), F32),
            pltpu.VMEM((teams, tile_rows, LANES), BF16),
            pltpu.VMEM((teams - 1, tile_rows, LANES), BF16),
            pltpu.SemaphoreType.DMA((rows // CHUNK,)),
            pltpu.SemaphoreType.DMA((3,)),
            pltpu.SemaphoreType.DMA((2,)),
            pltpu.SemaphoreType.DMA((2,)),
            pltpu.SemaphoreType.DMA((2,)),
            pltpu.SemaphoreType.DMA((teams - 1,)),
            pltpu.SemaphoreType.DMA((teams - 1,)),
        ],
        compiler_params=pltpu.CompilerParams(
            collective_id=0, has_side_effects=True, vmem_limit_bytes=52 * 2**20
        ),
        cost_estimate=pl.CostEstimate(
            flops=2 * rows * sites * made * (3 * width + 2 * sites),
            bytes_accessed=2 * rows * sites * (width + made),
            transcendentals=0,
        ),
    )(
        group_active_tallies,
        embedded_homologs,
        asking_projector.T,
        lookup_projector.T,
        content_projector.T,
        contact_inner_matrix,
        contact_inner_offset.reshape(1, features),
        contact_outer_matrix,
    )
    return (attended.transpose(0, 2, 1), pair.reshape(tile_rows, own_rows, outputs))


def solution(mesh):
    return jax.shard_map(
        body,
        mesh=mesh,
        in_specs=(
            P("depth", None, None),
            P("depth"),
            P(None, "head"),
            P(None, "head"),
            P(None, "head"),
            P(),
            P(),
            P(),
        ),
        out_specs=(P("depth", None, "head"), P("head", "depth", None)),
        check_vma=False,
    )
```

time: 374 us -> 49.3 us (0.13)
  waiting for transfers between devices: 205 us -> 0 us
  blocking collectives: 72 us -> 0 us
  matrix products: 40.2 us -> 0 us
  Pallas kernels: 0 us -> 37.6 us
  starting transfers between devices: 26.7 us -> 0 us
  between operations: 14.9 us -> 0.64 us
    psum x1 -> x0, waiting for transfers between devices: 205 us -> none  [body(): logits = lax.psum(partial_logits, 'depth')]
    psum x1 -> x0, blocking collectives: 72 us -> none  [body(): count = lax.psum(jnp.sum(group_active_tallies.astype(jnp.float32)), 'depth')]
    dot_general x7 -> x0, matrix products: 40.2 us -> none  [the longest x3 22.1 us: project(): jnp.dot(merged_matrix, weight, preferred_element_type=jnp.float32)]
    pallas_call x0 -> x1, Pallas kernels: none -> 37.6 us  [body(): pl.pallas_call(functools.partial(kernel, groups, teams), out_shape=(jax.S...]
    all_to_all x1 -> x0, starting transfers between devices: 26.7 us -> none  [body(): lax.all_to_all(tile, 'head', split_axis=1, concat_axis=0, tiled=True)]
    unnamed x19 -> x14, local copies, waits for them, and re-layouts: 8.99 us -> 9.92 us
  transfers between devices with their start and end apart: 2 -> 0, of which waited for: 1 -> 0; matrix products, arithmetic and copies ran while one was open for 5% -> 0% of each run, Pallas kernels for 0% -> 0%
where the time goes in v2:
time: 49.3 us; the launch traced here: 48.9 us
  Pallas kernels  37.6 us (76%)
  local copies, waits for them, and re-layouts  10.6 us (22%)
  between operations  0.64 us (1%)
    pallas_call x1, Pallas kernels, body(): pl.pallas_call(functools.partial(kernel, groups, teams), out_shape=(jax.S...  37.6 us
    unnamed x14, local copies, waits for them, and re-layouts  9.92 us

profile of v2, /device:TPU:1, one launch (start us, length us, event | category | flops | bytes accessed | tf_op | source)
XLA Modules:
  0.0 48.9 jit_solution(11990564268320770915)
XLA Ops:
  0.6 0.7 %reshape.10.offset = f32[1,288]{1,0:T(1,128)S(1)} reshape(f32[288]{0:T(512)} %param.14) | data formatting | bytes 2304 | tf_op jit(solution)/shard_map/reshape | solution.py:344
  1.3 0.0 copy-start
  1.3 1.0 %copy-done = f32[288,288]{1,0:T(8,128)S(1)} copy-done((f32[288,288]{1,0:T(8,128)S(1)}, f32[288,288]{1,0:T(8,128)}, u32[]{:S(2)}) %copy-start) | copy-done | bytes 331800
  2.3 0.0 copy-start.1
  2.3 1.0 %copy-done.1 = bf16[768,192]{0,1:T(8,128)(2,1)S(1)} copy-done((bf16[768,192]{0,1:T(8,128)(2,1)S(1)}, bf16[768,192]{0,1:T(8,128)(2,1)}, u32[]{:S(2)}) %copy-start.1) | copy-done | bytes 294936
  3.3 0.0 copy-start.2
  3.3 1.0 %copy-done.2 = bf16[768,192]{0,1:T(8,128)(2,1)S(1)} copy-done((bf16[768,192]{0,1:T(8,128)(2,1)S(1)}, bf16[768,192]{0,1:T(8,128)(2,1)}, u32[]{:S(2)}) %copy-start.2) | copy-done | bytes 294936
  4.3 0.0 copy-start.3
  4.3 1.0 %copy-done.3 = bf16[768,192]{0,1:T(8,128)(2,1)S(1)} copy-done((bf16[768,192]{0,1:T(8,128)(2,1)S(1)}, bf16[768,192]{0,1:T(8,128)(2,1)}, u32[]{:S(2)}) %copy-start.3) | copy-done | bytes 294936
  5.2 0.0 copy-start.4
  5.2 0.7 %copy-done.4 = f32[12,288]{1,0:T(8,128)S(1)} copy-done((f32[12,288]{1,0:T(8,128)S(1)}, f32[12,288]{1,0:T(8,128)}, u32[]{:S(2)}) %copy-start.4) | copy-done | bytes 13848
  6.0 0.0 copy-start.5
  6.0 0.7 %copy-done.5 = s32[4]{0:T(128)S(1)} copy-done((s32[4]{0:T(128)S(1)}, s32[4]{0:T(128)}, u32[]{:S(2)}) %copy-start.5) | copy-done | bytes 40
  6.6 37.6 %shard_map.95 = (bf16[32,192,256]{2,1,0:T(8,128)(2,1)}, bf16[512,288]{1,0:T(8,128)(2,1)S(1)}) custom-call(s32[4]{0:T(128)S(1)} %copy-done.5, bf16[32,256,768]{2,1,0:T(8,128)(2,1)} %x_hbm.1, bf16[192,768]{1,0:T(8,128)(2,1)S(1)} %bitcast.6, bf16[192,768]{1,0:T(8,128)(2,1)S(1)} %bitcast.7, bf16[192,768]{1,0:T(8,128)(2,1)S(1)} %bitcast.8, ...), custom_call_target="tpu_custom_call" | custom-call | flops 8858370048 | bytes 15728640 | tf_op jit(solution)/shard_map/pallas_call | solution.py:301
  44.3 3.9 %copy.12 = bf16[32,256,192]{1,2,0:T(8,128)(2,1)} copy(bf16[32,256,192]{1,2,0:T(8,128)(2,1)} %bitcast.9) | data formatting | bytes 6291456
  48.1 0.7 %copy.13 = bf16[64,8,288]{2,1,0:T(8,128)(2,1)} copy(bf16[64,8,288]{2,1,0:T(8,128)(2,1)S(1)} %bitcast.5) | data formatting | bytes 589824
Async XLA Ops:
  1.3 1.0 %copy-start = (f32[288,288]{1,0:T(8,128)S(1)}, f32[288,288]{1,0:T(8,128)}, u32[]{:S(2)}) copy-start(f32[288,288]{1,0:T(8,128)} %outer.1) | copy-start | bytes 995332
  2.3 1.0 %copy-start.1 = (bf16[768,192]{0,1:T(8,128)(2,1)S(1)}, bf16[768,192]{0,1:T(8,128)(2,1)}, u32[]{:S(2)}) copy-start(bf16[768,192]{0,1:T(8,128)(2,1)} %param.10) | copy-start | bytes 884740
  3.3 1.0 %copy-start.2 = (bf16[768,192]{0,1:T(8,128)(2,1)S(1)}, bf16[768,192]{0,1:T(8,128)(2,1)}, u32[]{:S(2)}) copy-start(bf16[768,192]{0,1:T(8,128)(2,1)} %param.11) | copy-start | bytes 884740
  4.3 1.0 %copy-start.3 = (bf16[768,192]{0,1:T(8,128)(2,1)S(1)}, bf16[768,192]{0,1:T(8,128)(2,1)}, u32[]{:S(2)}) copy-start(bf16[768,192]{0,1:T(8,128)(2,1)} %param.12) | copy-start | bytes 884740
  5.2 0.7 %copy-start.4 = (f32[12,288]{1,0:T(8,128)S(1)}, f32[12,288]{1,0:T(8,128)}, u32[]{:S(2)}) copy-start(f32[12,288]{1,0:T(8,128)} %inner.1) | copy-start | bytes 41476
  6.0 0.7 %copy-start.5 = (s32[4]{0:T(128)S(1)}, s32[4]{0:T(128)}, u32[]{:S(2)}) copy-start(s32[4]{0:T(128)} %tallies.1) | copy-start | bytes 52

commit v3 on v2

--- a/solution.py
+++ b/solution.py
@@ -30,16 +30,20 @@
 def kernel(
     groups,
     teams,
-    tallies,
+    tallies_hbm,
     x_hbm,
     wq_hbm,
     wk_hbm,
     wv_hbm,
+    inner_hbm,
+    offset_hbm,
+    outer_hbm,
+    attended,
+    pair,
+    tallies,
     inner,
     offset,
     outer,
-    attended,
-    pair,
     x,
     w,
     qs,
@@ -53,6 +57,7 @@
     tile_in,
     x_sem,
     w_sem,
+    small_sem,
     count_sem,
     sum_sem,
     map_sem,
@@ -81,6 +86,14 @@
     for c in range(steps):
         x_copy(c).start()
     w_copy(2).start()
+    small_copies = [
+        pltpu.make_async_copy(source, target, small_sem.at[n])
+        for n, (source, target) in enumerate(
+            [(tallies_hbm, tallies), (inner_hbm, inner), (offset_hbm, offset), (outer_hbm, outer)]
+        )
+    ]
+    for copy in small_copies:
+        copy.start()
 
     barrier = pltpu.get_barrier_semaphore()
 
@@ -92,6 +105,7 @@
     for k in range(1, teams):
         pl.semaphore_signal(barrier, inc=1, device_id=(me, lax.rem(team + k, teams)), device_id_type=pl.DeviceIdType.MESH)
 
+    small_copies[0].wait()
     w_copy(0).wait()
     w_copy(1).wait()
 
@@ -239,6 +253,8 @@
 
         lax.fori_loop(0, rows // 8, apply, 0)
 
+    for copy in small_copies[1:]:
+        copy.wait()
     inner_rows = jnp.concatenate(
         [
             jnp.broadcast_to(inner[...][:, None, :], (inner.shape[0], own_rows, inner.shape[1])).reshape(
@@ -262,7 +278,7 @@
     )
     feature = jnp.where(keep, spread, 0.0).reshape(tile_sites * own_rows, LANES).astype(BF16)
     plain = (((1,), (0,)), ((), ()))
-    before = dot(feature, inner_high, plain) + dot(feature, inner_low, plain) + offset[...]
+    before = dot(feature, inner_high, plain) + dot(feature, inner_low, plain) + offset[...][None, :]
     hidden_high, hidden_low = split_words(jax.nn.gelu(before))
     pair[...] = (
         dot(hidden_high, outer_high, plain)
@@ -292,11 +308,9 @@
     heads = made // HEAD_DIM
     groups, teams = lax.axis_size("depth"), lax.axis_size("head")
     own_rows = sites // groups
-    features = contact_inner_matrix.shape[1]
     outputs = contact_outer_matrix.shape[1]
     deep = heads * own_rows * (sites // LANES)
     tile_rows = sites // teams
-    anywhere = pl.BlockSpec(memory_space=pl.ANY)
     local = pl.BlockSpec(memory_space=pltpu.VMEM)
     attended, pair = pl.pallas_call(
         functools.partial(kernel, groups, teams),
@@ -304,9 +318,13 @@
             jax.ShapeDtypeStruct((rows, made, sites), BF16),
             jax.ShapeDtypeStruct((tile_rows * own_rows, outputs), BF16),
         ),
-        in_specs=[pl.BlockSpec(memory_space=pltpu.SMEM)] + [anywhere] * 4 + [local] * 3,
+        in_specs=[pl.BlockSpec(memory_space=pltpu.HBM)] * 8,
         out_specs=(local, local),
         scratch_shapes=[
+            pltpu.SMEM(group_active_tallies.shape, jnp.int32),
+            pltpu.VMEM(contact_inner_matrix.shape, F32),
+            pltpu.VMEM(contact_inner_offset.shape, F32),
+            pltpu.VMEM(contact_outer_matrix.shape, F32),
             pltpu.VMEM((rows, sites, width), BF16),
             pltpu.VMEM((3 * made, width), BF16),
             pltpu.VMEM((heads, rows * HEAD_DIM, sites), BF16),
@@ -320,6 +338,7 @@
             pltpu.VMEM((teams - 1, tile_rows, LANES), BF16),
             pltpu.SemaphoreType.DMA((rows // CHUNK,)),
             pltpu.SemaphoreType.DMA((3,)),
+            pltpu.SemaphoreType.DMA((4,)),
             pltpu.SemaphoreType.DMA((2,)),
             pltpu.SemaphoreType.DMA((2,)),
             pltpu.SemaphoreType.DMA((2,)),
@@ -327,7 +346,7 @@
             pltpu.SemaphoreType.DMA((teams - 1,)),
         ],
         compiler_params=pltpu.CompilerParams(
-            collective_id=0, has_side_effects=True, vmem_limit_bytes=52 * 2**20
+            collective_id=0, has_side_effects=True, vmem_limit_bytes=36 * 2**20
         ),
         cost_estimate=pl.CostEstimate(
             flops=2 * rows * sites * made * (3 * width + 2 * sites),
@@ -335,14 +354,19 @@
             transcendentals=0,
         ),
     )(
-        group_active_tallies,
-        embedded_homologs,
-        asking_projector.T,
-        lookup_projector.T,
-        content_projector.T,
-        contact_inner_matrix,
-        contact_inner_offset.reshape(1, features),
-        contact_outer_matrix,
+        *(
+            pltpu.with_memory_space_constraint(operand, pltpu.HBM)
+            for operand in (
+                group_active_tallies,
+                embedded_homologs,
+                asking_projector.T,
+                lookup_projector.T,
+                content_projector.T,
+                contact_inner_matrix,
+                contact_inner_offset,
+                contact_outer_matrix,
+            )
+        )
     )
     return (attended.transpose(0, 2, 1), pair.reshape(tile_rows, own_rows, outputs))
 

time: 49.3 us -> 41 us (0.83)
  local copies, waits for them, and re-layouts: 10.6 us -> 2.41 us
    unnamed x14 -> x2, local copies, waits for them, and re-layouts: 9.92 us -> 2.41 us
    reshape x1 -> x0, local copies, waits for them, and re-layouts: 0.68 us -> none  [body(): contact_inner_offset.reshape(1, features)]
where the time goes in v3:
time: 41 us; the launch traced here: 40.9 us
  Pallas kernels  37.8 us (92%)
  local copies, waits for them, and re-layouts  2.41 us (6%)
  between operations  0.64 us (2%)
    pallas_call x1, Pallas kernels, body(): pl.pallas_call(functools.partial(kernel, groups, teams), out_shape=(jax.S...  37.8 us
    unnamed x2, local copies, waits for them, and re-layouts  2.41 us

profile of v3, /device:TPU:1, one launch (start us, length us, event | category | flops | bytes accessed | tf_op | source)
XLA Modules:
  0.0 40.9 jit_solution(4541278017750463526)
XLA Ops:
  0.6 37.8 %shard_map.95 = (bf16[32,192,256]{2,1,0:T(8,128)(2,1)S(1)}, bf16[512,288]{1,0:T(8,128)(2,1)S(1)}) custom-call(s32[4]{0:T(128)} %tallies_hbm.1, bf16[32,256,768]{2,1,0:T(8,128)(2,1)} %x_hbm.1, bf16[192,768]{1,0:T(8,128)(2,1)} %bitcast.7, bf16[192,768]{1,0:T(8,128)(2,1)} %bitcast.8, bf16[192,768]{1,0:T(8,128)(2,1)} %bitcast.9, f32[12,288]{1,0:T(8,128)} %inner_hbm.1, ...), custom_call_target="tpu_custom_call" | custom-call | flops 8858370048 | bytes 15728640 | tf_op jit(solution)/shard_map/pallas_call | solution.py:315
  38.5 1.7 %copy.12 = bf16[32,256,192]{1,2,0:T(8,128)(2,1)} copy(bf16[32,256,192]{1,2,0:T(8,128)(2,1)S(1)} %bitcast.5) | data formatting | bytes 6291456
  40.1 0.7 %copy.13 = bf16[64,8,288]{2,1,0:T(8,128)(2,1)} copy(bf16[64,8,288]{2,1,0:T(8,128)(2,1)S(1)} %bitcast.6) | data formatting | bytes 589824

commit v4 on v3

v4 whole, which is shorter than its diff:
```python
import functools

import jax
import jax.numpy as jnp
import numpy as np
from jax import lax
from jax.experimental import pallas as pl
from jax.experimental.pallas import tpu as pltpu
from jax.sharding import PartitionSpec as P

HEAD_DIM = 64
BLOCK = 8
LANES = 128
PARTS = (4, 4, 8, 8, 8)

NT = (((1,), (1,)), ((), ()))
TN = (((0,), (0,)), ((), ()))
NN = (((1,), (0,)), ((), ()))
BOX = (4, 2, 4)
F32 = jnp.float32
BF16 = jnp.bfloat16


def dot(a, b, dims):
    return lax.dot_general(a, b, dims, preferred_element_type=F32)


def farthest_first(shape):
    offsets = [o for o in np.ndindex(*shape) if any(o)]
    return sorted(offsets, key=lambda o: -sum(min(a, n - a) for a, n in zip(o, shape)))


def split_words(a):
    high = a.astype(BF16)
    return high, (a - high.astype(F32)).astype(BF16)


def spread_kernel(
    groups,
    teams,
    tallies_hbm,
    x_hbm,
    wq_hbm,
    wk_hbm,
    wv_hbm,
    inner_hbm,
    outer_hbm,
    attended,
    flat,
    inner_words,
    outer_words,
    tallies,
    inner,
    outer,
    x,
    w,
    qs,
    ks,
    vs,
    sums,
    sums_in,
    maps_all,
    counts_near,
    counts_far,
    tile_out,
    tile_in,
    x_sem,
    w_sem,
    small_sem,
    near_sem,
    far_sem,
    sum_sem,
    map_sem,
    tile_send,
    tile_recv,
):
    rows, sites, width = x.shape
    made = w.shape[0] // 3
    heads = made // HEAD_DIM
    own_rows = sites // groups
    deep = own_rows * (sites // LANES)
    me = lax.axis_index("depth")
    team = lax.axis_index("head")
    place = (me // (BOX[1] * BOX[2]), lax.rem(me // BOX[2], BOX[1]), lax.rem(me, BOX[2]))

    def peer(offset):
        z, y, x_ = (lax.rem(a + o, n) if o else a for a, o, n in zip(place, offset, BOX))
        return (z * BOX[1] + y) * BOX[2] + x_

    peers = farthest_first(BOX)

    def remote(source, target, send_sem, recv_sem, to):
        return pltpu.make_async_remote_copy(
            src_ref=source,
            dst_ref=target,
            send_sem=send_sem,
            recv_sem=recv_sem,
            device_id=to,
            device_id_type=pl.DeviceIdType.MESH,
        )

    def wait_blocks(buffer, number, sem):
        most = buffer.at[pl.ds(0, number)]
        pltpu.make_async_copy(most, most, sem).wait()

    starts = [sum(PARTS[:n]) for n in range(len(PARTS))]

    def x_copy(n):
        part = pl.ds(starts[n], PARTS[n])
        return pltpu.make_async_copy(x_hbm.at[part], x.at[part], x_sem.at[n])

    def w_copy(n):
        return pltpu.make_async_copy(
            (wq_hbm, wk_hbm, wv_hbm)[n], w.at[pl.ds(n * made, made)], w_sem.at[n]
        )

    small_copies = [
        pltpu.make_async_copy(source, target, small_sem.at[n])
        for n, (source, target) in enumerate([(tallies_hbm, tallies), (inner_hbm, inner), (outer_hbm, outer)])
    ]
    w_copy(0).start()
    w_copy(1).start()
    small_copies[0].start()
    for n in range(len(PARTS)):
        x_copy(n).start()
    w_copy(2).start()
    small_copies[1].start()
    small_copies[2].start()

    barrier = pltpu.get_barrier_semaphore()

    def greet(k, carry):
        pl.semaphore_signal(barrier, inc=1, device_id=(lax.rem(me + k, groups), team), device_id_type=pl.DeviceIdType.MESH)
        return carry

    lax.fori_loop(1, groups, greet, 0)
    for k in range(1, teams):
        pl.semaphore_signal(barrier, inc=1, device_id=(me, lax.rem(team + k, teams)), device_id_type=pl.DeviceIdType.MESH)

    near_peers = [o for o in peers if o[0] == 0]
    far_peers = [o for o in peers if o[1] == 0 and o[2] == 0]

    def count_near_copy(n):
        return remote(
            counts_near.at[len(near_peers)], counts_near.at[n], near_sem.at[0], near_sem.at[1], (peer(near_peers[n]), team)
        )

    def count_far_copy(n):
        return remote(
            counts_far.at[len(far_peers)], counts_far.at[n], far_sem.at[0], far_sem.at[1], (peer(far_peers[n]), team)
        )

    small_copies[0].wait()
    w_copy(0).wait()
    w_copy(1).wait()
    for r in range(rows):
        if r in starts:
            x_copy(starts.index(r)).wait()
        if r == starts[-2]:
            count = jnp.float32(0)
            for n in range(rows // BLOCK):
                count += tallies[n].astype(F32)
            counts_near[len(near_peers)] = jnp.full(counts_near.shape[1:], count, F32)
            pl.semaphore_wait(barrier, groups - 1 + teams - 1)
            for n in range(len(near_peers)):
                count_near_copy(n).start()
        live = jnp.where(r % BLOCK < tallies[r // BLOCK], 1.0, 0.0)
        qk = dot(w[: 2 * made], x[r], NT)
        q = (qk[:made] * live).astype(BF16)
        k = qk[made:].astype(BF16)
        for h in range(heads):
            qs[h, r * HEAD_DIM : (r + 1) * HEAD_DIM, :] = q[h * HEAD_DIM : (h + 1) * HEAD_DIM]
            ks[h, r * HEAD_DIM : (r + 1) * HEAD_DIM, :] = k[h * HEAD_DIM : (h + 1) * HEAD_DIM]

    for h in range(heads):
        logits = dot(qs[h], ks[h], TN)
        halves = [
            logits[:, n * LANES : (n + 1) * LANES].reshape(groups, own_rows, LANES)
            for n in range(sites // LANES)
        ]
        sums[:, h * deep : (h + 1) * deep, :] = jnp.concatenate(halves, axis=1).astype(BF16)

    for n, offset in enumerate(peers):
        to = peer(offset)
        remote(sums.at[to], sums_in.at[n], sum_sem.at[0], sum_sem.at[1], (to, team)).start()

    wait_blocks(counts_near, len(near_peers), near_sem.at[1])
    counts_far[len(far_peers)] = jnp.sum(counts_near[...], axis=0)
    for n in range(len(far_peers)):
        count_far_copy(n).start()

    w_copy(2).wait()
    step = rows // 2

    def project_v(c, carry):
        for n in range(step):
            r = c * step + n
            v = dot(w[2 * made :], x[r], NT).astype(BF16)
            for h in range(heads):
                vs[h, pl.ds(r * HEAD_DIM, HEAD_DIM), :] = v[h * HEAD_DIM : (h + 1) * HEAD_DIM]
        return carry

    lax.fori_loop(0, rows // step, project_v, 0)

    wait_blocks(counts_far, len(far_peers), far_sem.at[1])
    scale = lax.rsqrt(HEAD_DIM * jnp.sum(counts_far[...], axis=0)[:1, :1])
    wait_blocks(sums_in, groups - 1, sum_sem.at[1])
    total = sums[me].astype(F32) + jnp.sum(sums_in[...].astype(F32), axis=0)
    blocks = []
    for h in range(heads):
        part = total[h * deep : (h + 1) * deep] * scale
        left, right = part[:own_rows], part[own_rows:]
        top = jnp.maximum(jnp.max(left, axis=1, keepdims=True), jnp.max(right, axis=1, keepdims=True))
        left, right = jnp.exp(left - top), jnp.exp(right - top)
        whole = jnp.sum(left, axis=1, keepdims=True) + jnp.sum(right, axis=1, keepdims=True)
        blocks += [left / whole, right / whole]
    maps_all[me] = jnp.concatenate(blocks, axis=0).astype(BF16)

    for offset in peers:
        remote(maps_all.at[me], maps_all.at[me], map_sem.at[0], map_sem.at[1], (peer(offset), team)).start()

    small_copies[1].wait()
    small_copies[2].wait()
    inner_rows = jnp.broadcast_to(inner[...][:, None, :], (inner.shape[0], own_rows, inner.shape[1]))
    inner_rows = inner_rows.reshape(inner.shape[0] * own_rows, inner.shape[1])
    inner_rows = jnp.concatenate(
        [inner_rows, jnp.zeros((LANES - inner_rows.shape[0], inner.shape[1]), F32)], axis=0
    )
    inner_words[0], inner_words[1] = split_words(inner_rows)
    outer_words[0], outer_words[1] = split_words(outer[...])

    wait_blocks(maps_all, groups - 1, map_sem.at[1])
    maps = []
    for h in range(heads):
        part = maps_all[:, h * deep : (h + 1) * deep, :].astype(F32)
        maps.append(
            jnp.concatenate(
                [part[:, :own_rows].reshape(sites, LANES), part[:, own_rows:].reshape(sites, LANES)], axis=1
            ).astype(BF16)
        )

    column = lax.broadcasted_iota(jnp.int32, (sites, LANES), 0) - me * own_rows
    lane = lax.broadcasted_iota(jnp.int32, (sites, LANES), 1)
    tile = jnp.zeros((sites, LANES), F32)
    for h in range(heads):
        spot = lane - (team * heads + h) * own_rows
        pick = (spot == column) & (spot >= 0) & (spot < own_rows)
        tile += dot(maps[h], pick.astype(F32).astype(BF16), NN)
    tile_out[...] = tile.astype(BF16).reshape(tile_out.shape)

    def tile_copy(k):
        to = lax.rem(team + k, teams)
        return remote(tile_out.at[to], tile_in.at[k - 1], tile_send.at[k - 1], tile_recv.at[k - 1], (me, to))

    for k in range(1, teams):
        tile_copy(k).start()

    for h in range(heads):
        out = dot(vs[h], maps[h], NT).astype(BF16)
        attended[:, h * HEAD_DIM : (h + 1) * HEAD_DIM, :] = out.reshape(rows, HEAD_DIM, sites)

    wait_blocks(counts_near, len(near_peers), near_sem.at[0])
    wait_blocks(counts_far, len(far_peers), far_sem.at[0])
    wait_blocks(sums_in, groups - 1, sum_sem.at[0])
    wait_blocks(maps_all, groups - 1, map_sem.at[0])
    joined = tile_out[team].astype(F32)
    for k in range(1, teams):
        tile_copy(k).wait_recv()
        joined += tile_in[k - 1].astype(F32)
    flat[...] = joined * sites
    for k in range(1, teams):
        tile_copy(k).wait_send()


def pair_kernel(own_rows, attended, flat, inner_words, outer_words, offset, attended_hbm, pair, out_sem):
    pieces = out_sem.shape[0]
    piece = attended.shape[0] // pieces
    copies = [
        pltpu.make_async_copy(
            attended.at[pl.ds(n * piece, piece)], attended_hbm.at[pl.ds(n * piece, piece)], out_sem.at[n]
        )
        for n in range(pieces)
    ]
    for copy in copies:
        copy.start()
    tile_rows = flat.shape[0]
    shape = (tile_rows, own_rows, LANES)
    keep = lax.rem(lax.broadcasted_iota(jnp.int32, shape, 2), own_rows) == lax.broadcasted_iota(jnp.int32, shape, 1)
    feature = jnp.where(keep, jnp.broadcast_to(flat[...][:, None, :], shape), 0.0)
    feature = feature.reshape(tile_rows * own_rows, LANES).astype(BF16)
    before = dot(feature, inner_words[0], NN) + dot(feature, inner_words[1], NN) + offset[...][None, :]
    high, low = split_words(jax.nn.gelu(before))
    pair[...] = (
        dot(high, outer_words[0], NN) + dot(low, outer_words[0], NN) + dot(high, outer_words[1], NN)
    ).astype(BF16)
    for copy in copies:
        copy.wait()


def body(
    embedded_homologs,
    group_active_tallies,
    asking_projector,
    lookup_projector,
    content_projector,
    contact_inner_matrix,
    contact_inner_offset,
    contact_outer_matrix,
):
    rows, sites, width = embedded_homologs.shape
    made = asking_projector.shape[1]
    heads = made // HEAD_DIM
    groups, teams = lax.axis_size("depth"), lax.axis_size("head")
    own_rows = sites // groups
    outputs = contact_outer_matrix.shape[1]
    deep = heads * own_rows * (sites // LANES)
    tile_rows = sites // teams
    local = pl.BlockSpec(memory_space=pltpu.VMEM)
    stacked = (heads, rows * HEAD_DIM, sites)
    attended, flat, inner_words, outer_words = pl.pallas_call(
        functools.partial(spread_kernel, groups, teams),
        out_shape=(
            jax.ShapeDtypeStruct((rows, made, sites), BF16),
            jax.ShapeDtypeStruct((tile_rows, LANES), F32),
            jax.ShapeDtypeStruct((2, LANES, contact_inner_matrix.shape[1]), BF16),
            jax.ShapeDtypeStruct((2,) + contact_outer_matrix.shape, BF16),
        ),
        in_specs=[pl.BlockSpec(memory_space=pltpu.HBM)] * 7,
        out_specs=(local,) * 4,
        scratch_shapes=[
            pltpu.SMEM(group_active_tallies.shape, jnp.int32),
            pltpu.VMEM(contact_inner_matrix.shape, F32),
            pltpu.VMEM(contact_outer_matrix.shape, F32),
            pltpu.VMEM((rows, sites, width), BF16),
            pltpu.VMEM((3 * made, width), BF16),
            pltpu.VMEM(stacked, BF16),
            pltpu.VMEM(stacked, BF16),
            pltpu.VMEM(stacked, BF16),
            pltpu.VMEM((groups, deep, LANES), BF16),
            pltpu.VMEM((groups - 1, deep, LANES), BF16),
            pltpu.VMEM((groups, deep, LANES), BF16),
            pltpu.VMEM((BOX[1] * BOX[2], 8, LANES), F32),
            pltpu.VMEM((BOX[0], 8, LANES), F32),
            pltpu.VMEM((teams, tile_rows, LANES), BF16),
            pltpu.VMEM((teams - 1, tile_rows, LANES), BF16),
            pltpu.SemaphoreType.DMA((len(PARTS),)),
            pltpu.SemaphoreType.DMA((3,)),
            pltpu.SemaphoreType.DMA((3,)),
            pltpu.SemaphoreType.DMA((2,)),
            pltpu.SemaphoreType.DMA((2,)),
            pltpu.SemaphoreType.DMA((2,)),
            pltpu.SemaphoreType.DMA((2,)),
            pltpu.SemaphoreType.DMA((teams - 1,)),
            pltpu.SemaphoreType.DMA((teams - 1,)),
        ],
        compiler_params=pltpu.CompilerParams(
            collective_id=0, has_side_effects=True, vmem_limit_bytes=36 * 2**20
        ),
        cost_estimate=pl.CostEstimate(
            flops=2 * rows * sites * made * (3 * width + 2 * sites),
            bytes_accessed=2 * rows * sites * (width + made),
            transcendentals=0,
        ),
    )(
        *(
            pltpu.with_memory_space_constraint(operand, pltpu.HBM)
            for operand in (
                group_active_tallies,
                embedded_homologs,
                asking_projector.T,
                lookup_projector.T,
                content_projector.T,
                contact_inner_matrix,
                contact_outer_matrix,
            )
        )
    )
    attended, pair = pl.pallas_call(
        functools.partial(pair_kernel, own_rows),
        out_shape=(
            jax.ShapeDtypeStruct(attended.shape, BF16),
            jax.ShapeDtypeStruct((tile_rows * own_rows, outputs), BF16),
        ),
        in_specs=[local] * 5,
        out_specs=(pl.BlockSpec(memory_space=pltpu.HBM), local),
        scratch_shapes=[pltpu.SemaphoreType.DMA((4,))],
        compiler_params=pltpu.CompilerParams(vmem_limit_bytes=16 * 2**20),
        cost_estimate=pl.CostEstimate(
            flops=2 * tile_rows * own_rows * outputs * outputs * 3,
            bytes_accessed=2 * rows * sites * made,
            transcendentals=tile_rows * own_rows * outputs,
        ),
    )(
        *(pltpu.with_memory_space_constraint(operand, pltpu.VMEM) for operand in (attended, flat, inner_words, outer_words)),
        contact_inner_offset,
    )
    return (attended.transpose(0, 2, 1), pair.reshape(tile_rows, own_rows, outputs))


def solution(mesh):
    return jax.shard_map(
        body,
        mesh=mesh,
        in_specs=(
            P("depth", None, None),
            P("depth"),
            P(None, "head"),
            P(None, "head"),
            P(None, "head"),
            P(),
            P(),
            P(),
        ),
        out_specs=(P("depth", None, "head"), P("head", "depth", None)),
        check_vma=False,
    )
```

time: 41 us -> 36.9 us (0.90)
  local copies, waits for them, and re-layouts: 2.41 us -> 0.01 us
  Pallas kernels: 37.8 us -> 36.2 us
    unnamed x2, local copies, waits for them, and re-layouts: 2.41 us -> 0.01 us
    pallas_call x1 -> x2, Pallas kernels: 37.8 us -> 36.2 us  [the longest x1 33.7 us: body(): pl.pallas_call(functools.partial(spread_kernel, groups, teams), out_shape...]
where the time goes in v4:
time: 36.9 us; the launch traced here: 36.8 us
  Pallas kernels  36.2 us (98%)
  between operations  0.66 us (2%)
    pallas_call x1, Pallas kernels, body(): pl.pallas_call(functools.partial(spread_kernel, groups, teams), out_shape...  33.7 us
    pallas_call x1, Pallas kernels, body(): pl.pallas_call(functools.partial(pair_kernel, own_rows), out_shape=(jax.S...  2.49 us

profile of v4, /device:TPU:1, one launch (start us, length us, event | category | flops | bytes accessed | tf_op | source)
XLA Modules:
  0.0 36.8 jit_solution(18364618458014614174)
XLA Ops:
  0.6 0.0 copy-start
  0.6 33.7 %shard_map.95 = (bf16[32,192,256]{2,1,0:T(8,128)(2,1)S(1)}, f32[64,128]{1,0:T(8,128)S(1)}, bf16[2,128,288]{2,1,0:T(8,128)(2,1)S(1)}, bf16[2,288,288]{2,1,0:T(8,128)(2,1)S(1)}) custom-call(s32[4]{0:T(128)} %tallies_hbm.1, bf16[32,256,768]{2,1,0:T(8,128)(2,1)} %x_hbm.1, bf16[192,768]{1,0:T(8,128)(2,1)} %bitcast.7, bf16[192,768]{1,0:T(8,128)(2,1)} %bitcast.8, ...), custom_call_target="tpu_custom_call" | custom-call | flops 8858370048 | bytes 15728640 | tf_op jit(solution)/shard_map/pallas_call | solution.py:320
  34.3 0.0 copy-done
  34.3 2.5 %shard_map.96 = (bf16[32,192,256]{2,1,0:T(8,128)(2,1)}, bf16[512,288]{1,0:T(8,128)(2,1)}) custom-call(bf16[32,192,256]{2,1,0:T(8,128)(2,1)S(1)} %get-tuple-element.8.attended, f32[64,128]{1,0:T(8,128)S(1)} %get-tuple-element.9.flat, bf16[2,128,288]{2,1,0:T(8,128)(2,1)S(1)} %get-tuple-element.10.inner_words, ...), custom_call_target="tpu_custom_call" | custom-call | flops 254803968 | bytes 3145728 | tf_op jit(solution)/shard_map/pallas_call | solution.py:378
Async XLA Ops:
  0.6 33.7 %copy-start = (f32[288]{0:T(512)S(1)}, f32[288]{0:T(512)}, u32[]{:S(2)}) copy-start(f32[288]{0:T(512)} %offset.1) | copy-start | bytes 3460

commit v5 on v4

--- a/solution.py
+++ b/solution.py
@@ -45,7 +45,8 @@
     wv_hbm,
     inner_hbm,
     outer_hbm,
-    attended,
+    vs,
+    maps,
     flat,
     inner_words,
     outer_words,
@@ -56,7 +57,6 @@
     w,
     qs,
     ks,
-    vs,
     sums,
     sums_in,
     maps_all,
@@ -71,8 +71,7 @@
     far_sem,
     sum_sem,
     map_sem,
-    tile_send,
-    tile_recv,
+    tile_sem,
 ):
     rows, sites, width = x.shape
     made = w.shape[0] // 3
@@ -81,6 +80,8 @@
     deep = own_rows * (sites // LANES)
     me = lax.axis_index("depth")
     team = lax.axis_index("head")
+    tile_groups = groups // teams
+    tile_team = me // tile_groups
     place = (me // (BOX[1] * BOX[2]), lax.rem(me // BOX[2], BOX[1]), lax.rem(me, BOX[2]))
 
     def peer(offset):
@@ -129,13 +130,16 @@
 
     barrier = pltpu.get_barrier_semaphore()
 
-    def greet(k, carry):
-        pl.semaphore_signal(barrier, inc=1, device_id=(lax.rem(me + k, groups), team), device_id_type=pl.DeviceIdType.MESH)
-        return carry
-
-    lax.fori_loop(1, groups, greet, 0)
-    for k in range(1, teams):
-        pl.semaphore_signal(barrier, inc=1, device_id=(me, lax.rem(team + k, teams)), device_id_type=pl.DeviceIdType.MESH)
+    def greet(to):
+        pl.semaphore_signal(barrier, inc=1, device_id=to, device_id_type=pl.DeviceIdType.MESH)
+
+    for offset in peers:
+        greet((peer(offset), team))
+
+    def greet_teams():
+        for n in range(tile_groups):
+            for k in range(1, teams):
+                greet((team * tile_groups + n, lax.rem(team + k, teams)))
 
     near_peers = [o for o in peers if o[0] == 0]
     far_peers = [o for o in peers if o[1] == 0 and o[2] == 0]
@@ -156,12 +160,14 @@
     for r in range(rows):
         if r in starts:
             x_copy(starts.index(r)).wait()
+        if r == starts[1]:
+            greet_teams()
         if r == starts[-2]:
             count = jnp.float32(0)
             for n in range(rows // BLOCK):
                 count += tallies[n].astype(F32)
             counts_near[len(near_peers)] = jnp.full(counts_near.shape[1:], count, F32)
-            pl.semaphore_wait(barrier, groups - 1 + teams - 1)
+            pl.semaphore_wait(barrier, jnp.where(tile_team == team, groups - 1, 2 * groups - 1))
             for n in range(len(near_peers)):
                 count_near_copy(n).start()
         live = jnp.where(r % BLOCK < tallies[r // BLOCK], 1.0, 0.0)
@@ -216,8 +222,46 @@
         blocks += [left / whole, right / whole]
     maps_all[me] = jnp.concatenate(blocks, axis=0).astype(BF16)
 
+    def spread_map(offset):
+        remote(maps_all.at[me], maps_all.at[me], map_sem.at[0], map_sem.at[1], (peer(offset), team)).start()
+
+    def spread_tile(offset):
+        to = peer(offset)
+        remote(
+            tile_out.at[to],
+            tile_in.at[team * tile_groups + lax.rem(me, tile_groups)],
+            tile_sem.at[0],
+            tile_sem.at[1],
+            (to, tile_team),
+        ).start()
+
     for offset in peers:
-        remote(maps_all.at[me], maps_all.at[me], map_sem.at[0], map_sem.at[1], (peer(offset), team)).start()
+        spread_map(offset)
+
+    shape = (groups, own_rows, sites)
+    keep = lax.broadcasted_iota(jnp.int32, shape, 2) // own_rows == lax.broadcasted_iota(jnp.int32, shape, 0)
+    column = lax.broadcasted_iota(jnp.int32, (sites, LANES), 0)
+    lane = lax.broadcasted_iota(jnp.int32, (sites, LANES), 1)
+    tile = jnp.zeros((sites, LANES), F32)
+    for h in range(heads):
+        both = jnp.concatenate([blocks[2 * h], blocks[2 * h + 1]], axis=1)
+        part = jnp.where(keep, jnp.broadcast_to(both[None], shape), 0.0).reshape(sites, sites).astype(BF16)
+        pick = lane - (team * heads + h) * own_rows == lax.rem(column, own_rows)
+        tile += dot(part, pick.astype(F32).astype(BF16), NN)
+    tile_out[...] = tile.reshape(tile_out.shape)
+    for offset in peers:
+        spread_tile(offset)
+    at_home = tile_team == team
+
+    @pl.when(jnp.logical_not(at_home))
+    def _():
+        spread_tile((0, 0, 0))
+
+    @pl.when(at_home)
+    def _():
+        pltpu.make_async_copy(
+            tile_out.at[me], tile_in.at[team * tile_groups + lax.rem(me, tile_groups)], tile_sem.at[1]
+        ).start()
 
     small_copies[1].wait()
     small_copies[2].wait()
@@ -230,59 +274,58 @@
     outer_words[0], outer_words[1] = split_words(outer[...])
 
     wait_blocks(maps_all, groups - 1, map_sem.at[1])
-    maps = []
     for h in range(heads):
         part = maps_all[:, h * deep : (h + 1) * deep, :].astype(F32)
-        maps.append(
-            jnp.concatenate(
-                [part[:, :own_rows].reshape(sites, LANES), part[:, own_rows:].reshape(sites, LANES)], axis=1
-            ).astype(BF16)
-        )
-
-    column = lax.broadcasted_iota(jnp.int32, (sites, LANES), 0) - me * own_rows
-    lane = lax.broadcasted_iota(jnp.int32, (sites, LANES), 1)
-    tile = jnp.zeros((sites, LANES), F32)
-    for h in range(heads):
-        spot = lane - (team * heads + h) * own_rows
-        pick = (spot == column) & (spot >= 0) & (spot < own_rows)
-        tile += dot(maps[h], pick.astype(F32).astype(BF16), NN)
-    tile_out[...] = tile.astype(BF16).reshape(tile_out.shape)
-
-    def tile_copy(k):
-        to = lax.rem(team + k, teams)
-        return remote(tile_out.at[to], tile_in.at[k - 1], tile_send.at[k - 1], tile_recv.at[k - 1], (me, to))
-
-    for k in range(1, teams):
-        tile_copy(k).start()
-
-    for h in range(heads):
-        out = dot(vs[h], maps[h], NT).astype(BF16)
-        attended[:, h * HEAD_DIM : (h + 1) * HEAD_DIM, :] = out.reshape(rows, HEAD_DIM, sites)
+        maps[h] = jnp.concatenate(
+            [part[:, :own_rows].reshape(sites, LANES), part[:, own_rows:].reshape(sites, LANES)], axis=1
+        ).astype(BF16)
+
+    wait_blocks(tile_in, groups, tile_sem.at[1])
+    flat[...] = jnp.sum(tile_in[...].reshape(teams, flat.shape[0], LANES), axis=0) * sites
 
     wait_blocks(counts_near, len(near_peers), near_sem.at[0])
     wait_blocks(counts_far, len(far_peers), far_sem.at[0])
     wait_blocks(sums_in, groups - 1, sum_sem.at[0])
     wait_blocks(maps_all, groups - 1, map_sem.at[0])
-    joined = tile_out[team].astype(F32)
-    for k in range(1, teams):
-        tile_copy(k).wait_recv()
-        joined += tile_in[k - 1].astype(F32)
-    flat[...] = joined * sites
-    for k in range(1, teams):
-        tile_copy(k).wait_send()
-
-
-def pair_kernel(own_rows, attended, flat, inner_words, outer_words, offset, attended_hbm, pair, out_sem):
-    pieces = out_sem.shape[0]
-    piece = attended.shape[0] // pieces
-    copies = [
-        pltpu.make_async_copy(
-            attended.at[pl.ds(n * piece, piece)], attended_hbm.at[pl.ds(n * piece, piece)], out_sem.at[n]
-        )
-        for n in range(pieces)
-    ]
-    for copy in copies:
-        copy.start()
+
+    @pl.when(jnp.logical_not(at_home))
+    def _():
+        wait_blocks(tile_out, groups, tile_sem.at[0])
+
+    @pl.when(at_home)
+    def _():
+        wait_blocks(tile_out, groups - 1, tile_sem.at[0])
+
+
+def apply_kernel(
+    own_rows,
+    vs,
+    maps,
+    flat,
+    inner_words,
+    outer_words,
+    offset,
+    attended_hbm,
+    pair_hbm,
+    attended,
+    pair,
+    out_sem,
+):
+    heads, _, sites = vs.shape
+    rows = attended.shape[0]
+
+    def apply(h):
+        part = slice(h * HEAD_DIM, (h + 1) * HEAD_DIM)
+        attended[:, part, :] = dot(vs[h], maps[h], NT).astype(BF16).reshape(rows, HEAD_DIM, sites)
+
+    def out_copy(h):
+        part = pl.ds(h * HEAD_DIM, HEAD_DIM)
+        return pltpu.make_async_copy(attended.at[:, part, :], attended_hbm.at[:, part, :], out_sem.at[h])
+
+    for h in range(heads - 1):
+        apply(h)
+        out_copy(h).start()
+
     tile_rows = flat.shape[0]
     shape = (tile_rows, own_rows, LANES)
     keep = lax.rem(lax.broadcasted_iota(jnp.int32, shape, 2), own_rows) == lax.broadcasted_iota(jnp.int32, shape, 1)
@@ -293,8 +336,13 @@
     pair[...] = (
         dot(high, outer_words[0], NN) + dot(low, outer_words[0], NN) + dot(high, outer_words[1], NN)
     ).astype(BF16)
-    for copy in copies:
-        copy.wait()
+    pair_copy = pltpu.make_async_copy(pair, pair_hbm, out_sem.at[heads])
+    pair_copy.start()
+    apply(heads - 1)
+    out_copy(heads - 1).start()
+    for h in range(heads):
+        out_copy(h).wait()
+    pair_copy.wait()
 
 
 def body(
@@ -317,16 +365,17 @@
     tile_rows = sites // teams
     local = pl.BlockSpec(memory_space=pltpu.VMEM)
     stacked = (heads, rows * HEAD_DIM, sites)
-    attended, flat, inner_words, outer_words = pl.pallas_call(
+    held = pl.pallas_call(
         functools.partial(spread_kernel, groups, teams),
         out_shape=(
-            jax.ShapeDtypeStruct((rows, made, sites), BF16),
+            jax.ShapeDtypeStruct(stacked, BF16),
+            jax.ShapeDtypeStruct((heads, sites, sites), BF16),
             jax.ShapeDtypeStruct((tile_rows, LANES), F32),
             jax.ShapeDtypeStruct((2, LANES, contact_inner_matrix.shape[1]), BF16),
             jax.ShapeDtypeStruct((2,) + contact_outer_matrix.shape, BF16),
         ),
         in_specs=[pl.BlockSpec(memory_space=pltpu.HBM)] * 7,
-        out_specs=(local,) * 4,
+        out_specs=(local,) * 5,
         scratch_shapes=[
             pltpu.SMEM(group_active_tallies.shape, jnp.int32),
             pltpu.VMEM(contact_inner_matrix.shape, F32),
@@ -335,14 +384,13 @@
             pltpu.VMEM((3 * made, width), BF16),
             pltpu.VMEM(stacked, BF16),
             pltpu.VMEM(stacked, BF16),
-            pltpu.VMEM(stacked, BF16),
             pltpu.VMEM((groups, deep, LANES), BF16),
             pltpu.VMEM((groups - 1, deep, LANES), BF16),
             pltpu.VMEM((groups, deep, LANES), BF16),
             pltpu.VMEM((BOX[1] * BOX[2], 8, LANES), F32),
             pltpu.VMEM((BOX[0], 8, LANES), F32),
-            pltpu.VMEM((teams, tile_rows, LANES), BF16),
-            pltpu.VMEM((teams - 1, tile_rows, LANES), BF16),
+            pltpu.VMEM((groups, own_rows, LANES), F32),
+            pltpu.VMEM((groups, own_rows, LANES), F32),
             pltpu.SemaphoreType.DMA((len(PARTS),)),
             pltpu.SemaphoreType.DMA((3,)),
             pltpu.SemaphoreType.DMA((3,)),
@@ -350,8 +398,7 @@
             pltpu.SemaphoreType.DMA((2,)),
             pltpu.SemaphoreType.DMA((2,)),
             pltpu.SemaphoreType.DMA((2,)),
-            pltpu.SemaphoreType.DMA((teams - 1,)),
-            pltpu.SemaphoreType.DMA((teams - 1,)),
+            pltpu.SemaphoreType.DMA((2,)),
         ],
         compiler_params=pltpu.CompilerParams(
             collective_id=0, has_side_effects=True, vmem_limit_bytes=36 * 2**20
@@ -376,22 +423,26 @@
         )
     )
     attended, pair = pl.pallas_call(
-        functools.partial(pair_kernel, own_rows),
+        functools.partial(apply_kernel, own_rows),
         out_shape=(
-            jax.ShapeDtypeStruct(attended.shape, BF16),
+            jax.ShapeDtypeStruct((rows, made, sites), BF16),
             jax.ShapeDtypeStruct((tile_rows * own_rows, outputs), BF16),
         ),
-        in_specs=[local] * 5,
-        out_specs=(pl.BlockSpec(memory_space=pltpu.HBM), local),
-        scratch_shapes=[pltpu.SemaphoreType.DMA((4,))],
+        in_specs=[local] * 6,
+        out_specs=(pl.BlockSpec(memory_space=pltpu.HBM),) * 2,
+        scratch_shapes=[
+            pltpu.VMEM((rows, made, sites), BF16),
+            pltpu.VMEM((tile_rows * own_rows, outputs), BF16),
+            pltpu.SemaphoreType.DMA((heads + 1,)),
+        ],
         compiler_params=pltpu.CompilerParams(vmem_limit_bytes=16 * 2**20),
         cost_estimate=pl.CostEstimate(
-            flops=2 * tile_rows * own_rows * outputs * outputs * 3,
+            flops=2 * rows * sites * made * sites,
             bytes_accessed=2 * rows * sites * made,
             transcendentals=tile_rows * own_rows * outputs,
         ),
     )(
-        *(pltpu.with_memory_space_constraint(operand, pltpu.VMEM) for operand in (attended, flat, inner_words, outer_words)),
+        *(pltpu.with_memory_space_constraint(operand, pltpu.VMEM) for operand in held),
         contact_inner_offset,
     )
     return (attended.transpose(0, 2, 1), pair.reshape(tile_rows, own_rows, outputs))

time: 36.9 us -> 37.4 us (1.014)
  Pallas kernels: 36.2 us -> 36.6 us
    pallas_call x1, Pallas kernels: 2.49 us -> 3.26 us  [body(): pl.pallas_call(functools.partial(apply_kernel, own_rows), out_shape=(jax....]
where the time goes in v5:
time: 37.4 us; the launch traced here: 37.3 us
  Pallas kernels  36.6 us (98%)
  between operations  0.66 us (2%)
    pallas_call x1, Pallas kernels, body(): pl.pallas_call(functools.partial(spread_kernel, groups, teams), out_shape...  33.4 us
    pallas_call x1, Pallas kernels, body(): pl.pallas_call(functools.partial(apply_kernel, own_rows), out_shape=(jax....  3.26 us

profile of v5, /device:TPU:1, one launch (start us, length us, event | category | flops | bytes accessed | tf_op | source)
XLA Modules:
  0.0 37.3 jit_solution(3472117300121253327)
XLA Ops:
  0.6 0.0 copy-start
  0.6 33.4 %shard_map.95 = (bf16[3,2048,256]{2,1,0:T(8,128)(2,1)S(1)}, bf16[3,256,256]{2,1,0:T(8,128)(2,1)S(1)}, f32[64,128]{1,0:T(8,128)S(1)}, bf16[2,128,288]{2,1,0:T(8,128)(2,1)S(1)}, bf16[2,288,288]{2,1,0:T(8,128)(2,1)S(1)}) custom-call(s32[4]{0:T(128)} %tallies_hbm.1, bf16[32,256,768]{2,1,0:T(8,128)(2,1)} %x_hbm.1, bf16[192,768]{1,0:T(8,128)(2,1)} %bitcast.7, ...), custom_call_target="tpu_custom_call" | custom-call | flops 8858370048 | bytes 15728640 | tf_op jit(solution)/shard_map/pallas_call | solution.py:368
  34.0 0.0 copy-done
  34.0 3.3 %shard_map.96 = (bf16[32,192,256]{2,1,0:T(8,128)(2,1)}, bf16[512,288]{1,0:T(8,128)(2,1)}) custom-call(bf16[3,2048,256]{2,1,0:T(8,128)(2,1)S(1)} %get-tuple-element.9.vs, bf16[3,256,256]{2,1,0:T(8,128)(2,1)S(1)} %get-tuple-element.10.maps, f32[64,128]{1,0:T(8,128)S(1)} %get-tuple-element.11.flat, bf16[2,128,288]{2,1,0:T(8,128)(2,1)S(1)} %get-tuple-element.12.inner_words, ...), custom_call_target="tpu_custom_call" | custom-call | flops 805306368 | bytes 3145728 | tf_op jit(solution)/shard_map/pallas_call | solution.py:425
Async XLA Ops:
  0.6 33.4 %copy-start = (f32[288]{0:T(512)S(1)}, f32[288]{0:T(512)}, u32[]{:S(2)}) copy-start(f32[288]{0:T(512)} %offset.1) | copy-start | bytes 3460

commit v6 on v5

--- a/solution.py
+++ b/solution.py
@@ -11,7 +11,7 @@
 HEAD_DIM = 64
 BLOCK = 8
 LANES = 128
-PARTS = (4, 4, 8, 8, 8)
+PARTS = (4, 8, 20)
 
 NT = (((1,), (1,)), ((), ()))
 TN = (((0,), (0,)), ((), ()))
@@ -49,7 +49,7 @@
     maps,
     flat,
     inner_words,
-    outer_words,
+    outer_word,
     tallies,
     inner,
     outer,
@@ -62,6 +62,7 @@
     maps_all,
     counts_near,
     counts_far,
+    picks,
     tile_out,
     tile_in,
     x_sem,
@@ -122,8 +123,8 @@
     w_copy(0).start()
     w_copy(1).start()
     small_copies[0].start()
-    for n in range(len(PARTS)):
-        x_copy(n).start()
+    x_copy(0).start()
+    x_copy(1).start()
     w_copy(2).start()
     small_copies[1].start()
     small_copies[2].start()
@@ -159,17 +160,12 @@
     w_copy(1).wait()
     for r in range(rows):
         if r in starts:
-            x_copy(starts.index(r)).wait()
-        if r == starts[1]:
-            greet_teams()
-        if r == starts[-2]:
-            count = jnp.float32(0)
-            for n in range(rows // BLOCK):
-                count += tallies[n].astype(F32)
-            counts_near[len(near_peers)] = jnp.full(counts_near.shape[1:], count, F32)
-            pl.semaphore_wait(barrier, jnp.where(tile_team == team, groups - 1, 2 * groups - 1))
-            for n in range(len(near_peers)):
-                count_near_copy(n).start()
+            n = starts.index(r)
+            x_copy(n).wait()
+            if n + 2 < len(PARTS):
+                x_copy(n + 2).start()
+            if n == 1:
+                greet_teams()
         live = jnp.where(r % BLOCK < tallies[r // BLOCK], 1.0, 0.0)
         qk = dot(w[: 2 * made], x[r], NT)
         q = (qk[:made] * live).astype(BF16)
@@ -178,6 +174,14 @@
             qs[h, r * HEAD_DIM : (r + 1) * HEAD_DIM, :] = q[h * HEAD_DIM : (h + 1) * HEAD_DIM]
             ks[h, r * HEAD_DIM : (r + 1) * HEAD_DIM, :] = k[h * HEAD_DIM : (h + 1) * HEAD_DIM]
 
+    count = jnp.float32(0)
+    for n in range(rows // BLOCK):
+        count += tallies[n].astype(F32)
+    counts_near[len(near_peers)] = jnp.full(counts_near.shape[1:], count, F32)
+    pl.semaphore_wait(barrier, jnp.where(tile_team == team, groups - 1, 2 * groups - 1))
+    for n in range(len(near_peers)):
+        count_near_copy(n).start()
+
     for h in range(heads):
         logits = dot(qs[h], ks[h], TN)
         halves = [
@@ -190,11 +194,6 @@
         to = peer(offset)
         remote(sums.at[to], sums_in.at[n], sum_sem.at[0], sum_sem.at[1], (to, team)).start()
 
-    wait_blocks(counts_near, len(near_peers), near_sem.at[1])
-    counts_far[len(far_peers)] = jnp.sum(counts_near[...], axis=0)
-    for n in range(len(far_peers)):
-        count_far_copy(n).start()
-
     w_copy(2).wait()
     step = rows // 2
 
@@ -204,9 +203,32 @@
             v = dot(w[2 * made :], x[r], NT).astype(BF16)
             for h in range(heads):
                 vs[h, pl.ds(r * HEAD_DIM, HEAD_DIM), :] = v[h * HEAD_DIM : (h + 1) * HEAD_DIM]
+
+        @pl.when(c == 0)
+        def _():
+            wait_blocks(counts_near, len(near_peers), near_sem.at[1])
+            counts_far[len(far_peers)] = jnp.sum(counts_near[...], axis=0)
+            for n in range(len(far_peers)):
+                count_far_copy(n).start()
+
         return carry
 
     lax.fori_loop(0, rows // step, project_v, 0)
+
+    small_copies[1].wait()
+    small_copies[2].wait()
+    inner_rows = jnp.broadcast_to(inner[...][:, None, :], (inner.shape[0], own_rows, inner.shape[1]))
+    inner_rows = inner_rows.reshape(inner.shape[0] * own_rows, inner.shape[1])
+    inner_rows = jnp.concatenate(
+        [inner_rows, jnp.zeros((LANES - inner_rows.shape[0], inner.shape[1]), F32)], axis=0
+    )
+    inner_words[:LANES], inner_words[LANES:] = split_words(inner_rows)
+    outer_word[...] = outer[...].astype(BF16)
+    column = lax.broadcasted_iota(jnp.int32, (sites, LANES), 0)
+    lane = lax.broadcasted_iota(jnp.int32, (sites, LANES), 1)
+    for h in range(heads):
+        pick = lane - (team * heads + h) * own_rows == lax.rem(column, own_rows)
+        picks[h] = pick.astype(F32).astype(BF16)
 
     wait_blocks(counts_far, len(far_peers), far_sem.at[1])
     scale = lax.rsqrt(HEAD_DIM * jnp.sum(counts_far[...], axis=0)[:1, :1])
@@ -235,22 +257,18 @@
             (to, tile_team),
         ).start()
 
-    for offset in peers:
-        spread_map(offset)
-
     shape = (groups, own_rows, sites)
     keep = lax.broadcasted_iota(jnp.int32, shape, 2) // own_rows == lax.broadcasted_iota(jnp.int32, shape, 0)
-    column = lax.broadcasted_iota(jnp.int32, (sites, LANES), 0)
-    lane = lax.broadcasted_iota(jnp.int32, (sites, LANES), 1)
     tile = jnp.zeros((sites, LANES), F32)
     for h in range(heads):
         both = jnp.concatenate([blocks[2 * h], blocks[2 * h + 1]], axis=1)
         part = jnp.where(keep, jnp.broadcast_to(both[None], shape), 0.0).reshape(sites, sites).astype(BF16)
-        pick = lane - (team * heads + h) * own_rows == lax.rem(column, own_rows)
-        tile += dot(part, pick.astype(F32).astype(BF16), NN)
+        tile += dot(part, picks[h], NN)
     tile_out[...] = tile.reshape(tile_out.shape)
+
     for offset in peers:
         spread_tile(offset)
+        spread_map(offset)
     at_home = tile_team == team
 
     @pl.when(jnp.logical_not(at_home))
@@ -262,16 +280,6 @@
         pltpu.make_async_copy(
             tile_out.at[me], tile_in.at[team * tile_groups + lax.rem(me, tile_groups)], tile_sem.at[1]
         ).start()
-
-    small_copies[1].wait()
-    small_copies[2].wait()
-    inner_rows = jnp.broadcast_to(inner[...][:, None, :], (inner.shape[0], own_rows, inner.shape[1]))
-    inner_rows = inner_rows.reshape(inner.shape[0] * own_rows, inner.shape[1])
-    inner_rows = jnp.concatenate(
-        [inner_rows, jnp.zeros((LANES - inner_rows.shape[0], inner.shape[1]), F32)], axis=0
-    )
-    inner_words[0], inner_words[1] = split_words(inner_rows)
-    outer_words[0], outer_words[1] = split_words(outer[...])
 
     wait_blocks(maps_all, groups - 1, map_sem.at[1])
     for h in range(heads):
@@ -303,7 +311,7 @@
     maps,
     flat,
     inner_words,
-    outer_words,
+    outer_word,
     offset,
     attended_hbm,
     pair_hbm,
@@ -322,7 +330,7 @@
         part = pl.ds(h * HEAD_DIM, HEAD_DIM)
         return pltpu.make_async_copy(attended.at[:, part, :], attended_hbm.at[:, part, :], out_sem.at[h])
 
-    for h in range(heads - 1):
+    for h in range(heads):
         apply(h)
         out_copy(h).start()
 
@@ -331,15 +339,11 @@
     keep = lax.rem(lax.broadcasted_iota(jnp.int32, shape, 2), own_rows) == lax.broadcasted_iota(jnp.int32, shape, 1)
     feature = jnp.where(keep, jnp.broadcast_to(flat[...][:, None, :], shape), 0.0)
     feature = feature.reshape(tile_rows * own_rows, LANES).astype(BF16)
-    before = dot(feature, inner_words[0], NN) + dot(feature, inner_words[1], NN) + offset[...][None, :]
-    high, low = split_words(jax.nn.gelu(before))
-    pair[...] = (
-        dot(high, outer_words[0], NN) + dot(low, outer_words[0], NN) + dot(high, outer_words[1], NN)
-    ).astype(BF16)
+    feature = jnp.concatenate([feature, feature], axis=1)
+    before = dot(feature, inner_words[...], NN) + offset[...][None, :]
+    pair[...] = dot(jax.nn.gelu(before).astype(BF16), outer_word[...], NN).astype(BF16)
     pair_copy = pltpu.make_async_copy(pair, pair_hbm, out_sem.at[heads])
     pair_copy.start()
-    apply(heads - 1)
-    out_copy(heads - 1).start()
     for h in range(heads):
         out_copy(h).wait()
     pair_copy.wait()
@@ -371,8 +375,8 @@
             jax.ShapeDtypeStruct(stacked, BF16),
             jax.ShapeDtypeStruct((heads, sites, sites), BF16),
             jax.ShapeDtypeStruct((tile_rows, LANES), F32),
-            jax.ShapeDtypeStruct((2, LANES, contact_inner_matrix.shape[1]), BF16),
-            jax.ShapeDtypeStruct((2,) + contact_outer_matrix.shape, BF16),
+            jax.ShapeDtypeStruct((2 * LANES, contact_inner_matrix.shape[1]), BF16),
+            jax.ShapeDtypeStruct(contact_outer_matrix.shape, BF16),
         ),
         in_specs=[pl.BlockSpec(memory_space=pltpu.HBM)] * 7,
         out_specs=(local,) * 5,
@@ -389,6 +393,7 @@
             pltpu.VMEM((groups, deep, LANES), BF16),
             pltpu.VMEM((BOX[1] * BOX[2], 8, LANES), F32),
             pltpu.VMEM((BOX[0], 8, LANES), F32),
+            pltpu.VMEM((heads, sites, LANES), BF16),
             pltpu.VMEM((groups, own_rows, LANES), F32),
             pltpu.VMEM((groups, own_rows, LANES), F32),
             pltpu.SemaphoreType.DMA((len(PARTS),)),

time: 37.4 us -> 35.6 us (0.952)
  Pallas kernels: 36.6 us -> 34.8 us
    pallas_call x1, Pallas kernels: 33.4 us -> 32.3 us  [body(): pl.pallas_call(functools.partial(spread_kernel, groups, teams), out_shape...]
    pallas_call x1, Pallas kernels: 3.26 us -> 2.56 us  [body(): pl.pallas_call(functools.partial(apply_kernel, own_rows), out_shape=(jax....]
where the time goes in v6:
time: 35.6 us; the launch traced here: 35.5 us
  Pallas kernels  34.8 us (98%)
  between operations  0.66 us (2%)
    pallas_call x1, Pallas kernels, body(): pl.pallas_call(functools.partial(spread_kernel, groups, teams), out_shape...  32.3 us
    pallas_call x1, Pallas kernels, body(): pl.pallas_call(functools.partial(apply_kernel, own_rows), out_shape=(jax....  2.56 us

profile of v6, /device:TPU:1, one launch (start us, length us, event | category | flops | bytes accessed | tf_op | source)
XLA Modules:
  0.0 35.5 jit_solution(15284684966803150947)
XLA Ops:
  0.6 0.0 copy-start
  0.6 32.3 %shard_map.95 = (bf16[3,2048,256]{2,1,0:T(8,128)(2,1)S(1)}, bf16[3,256,256]{2,1,0:T(8,128)(2,1)S(1)}, f32[64,128]{1,0:T(8,128)S(1)}, bf16[256,288]{1,0:T(8,128)(2,1)S(1)}, bf16[288,288]{1,0:T(8,128)(2,1)S(1)}) custom-call(s32[4]{0:T(128)} %tallies_hbm.1, bf16[32,256,768]{2,1,0:T(8,128)(2,1)} %x_hbm.1, bf16[192,768]{1,0:T(8,128)(2,1)} %bitcast.7, ...), custom_call_target="tpu_custom_call" | custom-call | flops 8858370048 | bytes 15728640 | tf_op jit(solution)/shard_map/pallas_call | solution.py:372
  32.9 0.0 copy-done
  32.9 2.6 %shard_map.96 = (bf16[32,192,256]{2,1,0:T(8,128)(2,1)}, bf16[512,288]{1,0:T(8,128)(2,1)}) custom-call(bf16[3,2048,256]{2,1,0:T(8,128)(2,1)S(1)} %get-tuple-element.9.vs, bf16[3,256,256]{2,1,0:T(8,128)(2,1)S(1)} %get-tuple-element.10.maps, f32[64,128]{1,0:T(8,128)S(1)} %get-tuple-element.11.flat, bf16[256,288]{1,0:T(8,128)(2,1)S(1)} %get-tuple-element.12.inner_words, ...), custom_call_target="tpu_custom_call" | custom-call | flops 805306368 | bytes 3145728 | tf_op jit(solution)/shard_map/pallas_call | solution.py:430
Async XLA Ops:
  0.6 32.3 %copy-start = (f32[288]{0:T(512)S(1)}, f32[288]{0:T(512)}, u32[]{:S(2)}) copy-start(f32[288]{0:T(512)} %offset.1) | copy-start | bytes 3460

commit v7 on v6

--- a/solution.py
+++ b/solution.py
@@ -16,6 +16,8 @@
 NT = (((1,), (1,)), ((), ()))
 TN = (((0,), (0,)), ((), ()))
 NN = (((1,), (0,)), ((), ()))
+HALVES = 2
+SLOT = 32
 BOX = (4, 2, 4)
 F32 = jnp.float32
 BF16 = jnp.bfloat16
@@ -63,6 +65,7 @@
     counts_near,
     counts_far,
     picks,
+    moves,
     tile_out,
     tile_in,
     x_sem,
@@ -224,11 +227,19 @@
     )
     inner_words[:LANES], inner_words[LANES:] = split_words(inner_rows)
     outer_word[...] = outer[...].astype(BF16)
-    column = lax.broadcasted_iota(jnp.int32, (sites, LANES), 0)
-    lane = lax.broadcasted_iota(jnp.int32, (sites, LANES), 1)
-    for h in range(heads):
-        pick = lane - (team * heads + h) * own_rows == lax.rem(column, own_rows)
+    pairs = own_rows // 2
+    shape = (pairs * sites, LANES)
+    column = lax.broadcasted_iota(jnp.int32, shape, 0)
+    lane = lax.broadcasted_iota(jnp.int32, shape, 1)
+    for h in range(heads):
+        pick = lane == column // sites * SLOT + h * own_rows + lax.rem(column, own_rows)
         picks[h] = pick.astype(F32).astype(BF16)
+    shape = (teams * LANES, LANES)
+    column = lax.broadcasted_iota(jnp.int32, shape, 0)
+    lane = lax.broadcasted_iota(jnp.int32, shape, 1)
+    slot = lax.rem(column, SLOT)
+    pick = (lane == column // LANES * (heads * own_rows) + slot) & (slot < heads * own_rows)
+    moves[...] = pick.astype(F32).astype(BF16)
 
     wait_blocks(counts_far, len(far_peers), far_sem.at[1])
     scale = lax.rsqrt(HEAD_DIM * jnp.sum(counts_far[...], axis=0)[:1, :1])
@@ -257,17 +268,32 @@
             (to, tile_team),
         ).start()
 
-    shape = (groups, own_rows, sites)
-    keep = lax.broadcasted_iota(jnp.int32, shape, 2) // own_rows == lax.broadcasted_iota(jnp.int32, shape, 0)
-    tile = jnp.zeros((sites, LANES), F32)
+    per = own_rows // 2
+    shape = (groups // per, own_rows, pairs * sites)
+    owner = lax.broadcasted_iota(jnp.int32, shape, 0) * per + lax.broadcasted_iota(jnp.int32, shape, 1) // 2
+    keep = lax.rem(lax.broadcasted_iota(jnp.int32, shape, 2), sites) // own_rows == owner
+    odd = lax.rem(lax.broadcasted_iota(jnp.int32, (own_rows, sites), 0), 2) == 1
+    tile = jnp.zeros((2 * groups, LANES), F32)
     for h in range(heads):
         both = jnp.concatenate([blocks[2 * h], blocks[2 * h + 1]], axis=1)
-        part = jnp.where(keep, jnp.broadcast_to(both[None], shape), 0.0).reshape(sites, sites).astype(BF16)
-        tile += dot(part, picks[h], NN)
+        wide = jnp.concatenate(
+            [
+                jnp.where(
+                    odd,
+                    jnp.broadcast_to(both[2 * n + 1 : 2 * n + 2], odd.shape),
+                    jnp.broadcast_to(both[2 * n : 2 * n + 1], odd.shape),
+                )
+                for n in range(pairs)
+            ],
+            axis=1,
+        )
+        part = jnp.where(keep, jnp.broadcast_to(wide[None], shape), 0.0)
+        tile += dot(part.reshape(2 * groups, pairs * sites).astype(BF16), picks[h], NN)
     tile_out[...] = tile.reshape(tile_out.shape)
 
     for offset in peers:
         spread_tile(offset)
+    for offset in peers:
         spread_map(offset)
     at_home = tile_team == team
 
@@ -289,7 +315,19 @@
         ).astype(BF16)
 
     wait_blocks(tile_in, groups, tile_sem.at[1])
-    flat[...] = jnp.sum(tile_in[...].reshape(teams, flat.shape[0], LANES), axis=0) * sites
+    shape = (tile_groups, own_rows, LANES)
+    row = lax.broadcasted_iota(jnp.int32, shape, 1)
+    keep = lax.broadcasted_iota(jnp.int32, shape, 2) // SLOT == row // 2
+    parts = []
+    for n in range(teams):
+        part = tile_in[n * tile_groups : (n + 1) * tile_groups]
+        part = jnp.where(
+            lax.rem(row, 2) == 1,
+            jnp.broadcast_to(part[:, 1:2], shape),
+            jnp.broadcast_to(part[:, 0:1], shape),
+        )
+        parts.append(jnp.where(keep, part, 0.0).reshape(flat.shape).astype(BF16))
+    flat[...] = dot(jnp.concatenate(parts, axis=1), moves[...], NN) * sites
 
     wait_blocks(counts_near, len(near_peers), near_sem.at[0])
     wait_blocks(counts_far, len(far_peers), far_sem.at[0])
@@ -334,19 +372,28 @@
         apply(h)
         out_copy(h).start()
 
-    tile_rows = flat.shape[0]
+    halves = out_sem.shape[0] - heads
+    tile_rows = flat.shape[0] // halves
     shape = (tile_rows, own_rows, LANES)
     keep = lax.rem(lax.broadcasted_iota(jnp.int32, shape, 2), own_rows) == lax.broadcasted_iota(jnp.int32, shape, 1)
-    feature = jnp.where(keep, jnp.broadcast_to(flat[...][:, None, :], shape), 0.0)
-    feature = feature.reshape(tile_rows * own_rows, LANES).astype(BF16)
-    feature = jnp.concatenate([feature, feature], axis=1)
-    before = dot(feature, inner_words[...], NN) + offset[...][None, :]
-    pair[...] = dot(jax.nn.gelu(before).astype(BF16), outer_word[...], NN).astype(BF16)
-    pair_copy = pltpu.make_async_copy(pair, pair_hbm, out_sem.at[heads])
-    pair_copy.start()
+
+    def pair_copy(n):
+        part = pl.ds(n * tile_rows * own_rows, tile_rows * own_rows)
+        return pltpu.make_async_copy(pair.at[part], pair_hbm.at[part], out_sem.at[heads + n])
+
+    for n in range(halves):
+        rows_here = flat[n * tile_rows : (n + 1) * tile_rows]
+        feature = jnp.where(keep, jnp.broadcast_to(rows_here[:, None, :], shape), 0.0)
+        feature = feature.reshape(tile_rows * own_rows, LANES).astype(BF16)
+        feature = jnp.concatenate([feature, feature], axis=1)
+        before = dot(feature, inner_words[...], NN) + offset[...][None, :]
+        out = dot(jax.nn.gelu(before).astype(BF16), outer_word[...], NN).astype(BF16)
+        pair[n * tile_rows * own_rows : (n + 1) * tile_rows * own_rows] = out
+        pair_copy(n).start()
     for h in range(heads):
         out_copy(h).wait()
-    pair_copy.wait()
+    for n in range(halves):
+        pair_copy(n).wait()
 
 
 def body(
@@ -393,9 +440,10 @@
             pltpu.VMEM((groups, deep, LANES), BF16),
             pltpu.VMEM((BOX[1] * BOX[2], 8, LANES), F32),
             pltpu.VMEM((BOX[0], 8, LANES), F32),
-            pltpu.VMEM((heads, sites, LANES), BF16),
-            pltpu.VMEM((groups, own_rows, LANES), F32),
-            pltpu.VMEM((groups, own_rows, LANES), F32),
+            pltpu.VMEM((heads, own_rows // 2 * sites, LANES), BF16),
+            pltpu.VMEM((teams * LANES, LANES), BF16),
+            pltpu.VMEM((groups, 2, LANES), F32),
+            pltpu.VMEM((groups, 2, LANES), F32),
             pltpu.SemaphoreType.DMA((len(PARTS),)),
             pltpu.SemaphoreType.DMA((3,)),
             pltpu.SemaphoreType.DMA((3,)),
@@ -438,7 +486,7 @@
         scratch_shapes=[
             pltpu.VMEM((rows, made, sites), BF16),
             pltpu.VMEM((tile_rows * own_rows, outputs), BF16),
-            pltpu.SemaphoreType.DMA((heads + 1,)),
+            pltpu.SemaphoreType.DMA((heads + HALVES,)),
         ],
         compiler_params=pltpu.CompilerParams(vmem_limit_bytes=16 * 2**20),
         cost_estimate=pl.CostEstimate(

time: 35.6 us -> 33.8 us (0.949)
  the two profiles are of different devices: /device:TPU:1 before, /device:TPU:0 now
where the time goes in v7:
time: 33.8 us; the launch traced here: 33.7 us
  Pallas kernels  33 us (98%)
  between operations  0.66 us (2%)
    pallas_call x1, Pallas kernels, body(): pl.pallas_call(functools.partial(spread_kernel, groups, teams), out_shape...  30.4 us
    pallas_call x1, Pallas kernels, body(): pl.pallas_call(functools.partial(apply_kernel, own_rows), out_shape=(jax....  2.56 us

profile of v7, /device:TPU:0, one launch (start us, length us, event | category | flops | bytes accessed | tf_op | source)
XLA Modules:
  0.0 33.7 jit_solution(14391612521080917002)
XLA Ops:
  0.6 0.0 copy-start
  0.6 30.4 %shard_map.95 = (bf16[3,2048,256]{2,1,0:T(8,128)(2,1)S(1)}, bf16[3,256,256]{2,1,0:T(8,128)(2,1)S(1)}, f32[64,128]{1,0:T(8,128)S(1)}, bf16[256,288]{1,0:T(8,128)(2,1)S(1)}, bf16[288,288]{1,0:T(8,128)(2,1)S(1)}) custom-call(s32[4]{0:T(128)} %tallies_hbm.1, bf16[32,256,768]{2,1,0:T(8,128)(2,1)} %x_hbm.1, bf16[192,768]{1,0:T(8,128)(2,1)} %bitcast.7, ...), custom_call_target="tpu_custom_call" | custom-call | flops 8858370048 | bytes 15728640 | tf_op jit(solution)/shard_map/pallas_call | solution.py:419
  31.1 0.0 copy-done
  31.1 2.6 %shard_map.96 = (bf16[32,192,256]{2,1,0:T(8,128)(2,1)}, bf16[512,288]{1,0:T(8,128)(2,1)}) custom-call(bf16[3,2048,256]{2,1,0:T(8,128)(2,1)S(1)} %get-tuple-element.9.vs, bf16[3,256,256]{2,1,0:T(8,128)(2,1)S(1)} %get-tuple-element.10.maps, f32[64,128]{1,0:T(8,128)S(1)} %get-tuple-element.11.flat, bf16[256,288]{1,0:T(8,128)(2,1)S(1)} %get-tuple-element.12.inner_words, ...), custom_call_target="tpu_custom_call" | custom-call | flops 805306368 | bytes 3145728 | tf_op jit(solution)/shard_map/pallas_call | solution.py:478
Async XLA Ops:
  0.6 30.5 %copy-start = (f32[288]{0:T(512)S(1)}, f32[288]{0:T(512)}, u32[]{:S(2)}) copy-start(f32[288]{0:T(512)} %offset.1) | copy-start | bytes 3460

commit v8 on v7

--- a/solution.py
+++ b/solution.py
@@ -11,11 +11,12 @@
 HEAD_DIM = 64
 BLOCK = 8
 LANES = 128
-PARTS = (4, 8, 20)
+PARTS = (4, 14, 14)
 
 NT = (((1,), (1,)), ((), ()))
 TN = (((0,), (0,)), ((), ()))
 NN = (((1,), (0,)), ((), ()))
+EARLY = 6
 HALVES = 2
 SLOT = 32
 BOX = (4, 2, 4)
@@ -268,6 +269,9 @@
             (to, tile_team),
         ).start()
 
+    for offset in peers[:EARLY]:
+        spread_map(offset)
+
     per = own_rows // 2
     shape = (groups // per, own_rows, pairs * sites)
     owner = lax.broadcasted_iota(jnp.int32, shape, 0) * per + lax.broadcasted_iota(jnp.int32, shape, 1) // 2
@@ -293,7 +297,7 @@
 
     for offset in peers:
         spread_tile(offset)
-    for offset in peers:
+    for offset in peers[EARLY:]:
         spread_map(offset)
     at_home = tile_team == team
 

time: 33.8 us -> 32.9 us (0.973)
  the two profiles are of different devices: /device:TPU:0 before, /device:TPU:1 now
where the time goes in v8:
time: 32.9 us; the launch traced here: 32.5 us
  Pallas kernels  31.8 us (97%)
  between operations  0.66 us (2%)
    pallas_call x1, Pallas kernels, body(): pl.pallas_call(functools.partial(spread_kernel, groups, teams), out_shape...  29.3 us
    pallas_call x1, Pallas kernels, body(): pl.pallas_call(functools.partial(apply_kernel, own_rows), out_shape=(jax....  2.56 us

profile of v8, /device:TPU:1, one launch (start us, length us, event | category | flops | bytes accessed | tf_op | source)
XLA Modules:
  0.0 32.5 jit_solution(2173452182014603250)
XLA Ops:
  0.6 0.0 copy-start
  0.6 29.3 %shard_map.95 = (bf16[3,2048,256]{2,1,0:T(8,128)(2,1)S(1)}, bf16[3,256,256]{2,1,0:T(8,128)(2,1)S(1)}, f32[64,128]{1,0:T(8,128)S(1)}, bf16[256,288]{1,0:T(8,128)(2,1)S(1)}, bf16[288,288]{1,0:T(8,128)(2,1)S(1)}) custom-call(s32[4]{0:T(128)} %tallies_hbm.1, bf16[32,256,768]{2,1,0:T(8,128)(2,1)} %x_hbm.1, bf16[192,768]{1,0:T(8,128)(2,1)} %bitcast.7, ...), custom_call_target="tpu_custom_call" | custom-call | flops 8858370048 | bytes 15728640 | tf_op jit(solution)/shard_map/pallas_call | solution.py:423
  29.9 0.0 copy-done
  29.9 2.6 %shard_map.96 = (bf16[32,192,256]{2,1,0:T(8,128)(2,1)}, bf16[512,288]{1,0:T(8,128)(2,1)}) custom-call(bf16[3,2048,256]{2,1,0:T(8,128)(2,1)S(1)} %get-tuple-element.9.vs, bf16[3,256,256]{2,1,0:T(8,128)(2,1)S(1)} %get-tuple-element.10.maps, f32[64,128]{1,0:T(8,128)S(1)} %get-tuple-element.11.flat, bf16[256,288]{1,0:T(8,128)(2,1)S(1)} %get-tuple-element.12.inner_words, ...), custom_call_target="tpu_custom_call" | custom-call | flops 805306368 | bytes 3145728 | tf_op jit(solution)/shard_map/pallas_call | solution.py:482
Async XLA Ops:
  0.6 29.3 %copy-start = (f32[288]{0:T(512)S(1)}, f32[288]{0:T(512)}, u32[]{:S(2)}) copy-start(f32[288]{0:T(512)} %offset.1) | copy-start | bytes 3460
